TPU v7x, 128 devices: a whole 4x4x4 slice. The times are simulated.
128 devices in a mesh: band: 32 (over z, x, y_lo), space: 4 (over y_hi, core).
Axes of the slice: x: 4, y: 4 (y_hi: 2, y_lo: 2; y = y_hi * 2 + y_lo), z: 4, core: 2. Of those that a mesh axis runs over, the one named last changes fastest.
Arguments:
- panels: float32 [3, 64, 32, 128, 128], P(None, 'band', 'space'), may hold values from -6 to 6
- potential: float32 [32, 128, 128], P('space'), may hold values from -8 to 0
- block_index: int32 [1], replicated, may hold values from 0 to 2
Outputs:
- filtered: float32 [64, 32, 128, 128], P('band', 'space')
- updated: float32 [3, 64, 32, 128, 128], P(None, 'band', 'space')
All inputs are finite; a program needn't handle non-finite values.
Results may differ from a plain program's by a relative error of at most 0.000071.
Values sent between devices are 32-bit elements; how exact they have to be, the bound alone decides.
No kernel may reach another device: no remote copies, remote signals or barrier semaphores. Data moves between devices by JAX's collectives and lax.ppermute only.
A program may use at most 192 MiB of HBM per device.

v0:
```python
import jax
import jax.numpy as jnp
from jax import lax
from jax.sharding import PartitionSpec as P

stencil_weights = (
    -5369.0 / 1800.0,
    12.0 / 7.0,
    -15.0 / 56.0,
    10.0 / 189.0,
    -1.0 / 112.0,
    2.0 / 1925.0,
    -1.0 / 16632.0,
)
stencil_reach = 6
kinetic_factor = -0.5 / 0.25
centre_value = 32.25
half_width = 10.75


def padded_2(shard, sides, width):
    for axis, dim in sides:
        size, length = (lax.axis_size(axis), shard.shape[dim])
        up = [(i, (i + 1) % size) for i in range(size)]
        down = [(j, i) for i, j in up]
        last = lax.slice_in_dim(shard, length - width, length, axis=dim)
        initial = lax.slice_in_dim(shard, 0, width, axis=dim)
        before = lax.ppermute(last, axis, up)
        after = lax.ppermute(initial, axis, down)
        shard = jnp.concatenate([before, shard, after], axis=dim)
    return shard


def hamiltonian(padded, potential):
    plane_count = padded.shape[1] - 2 * stencil_reach
    centre = padded[:, stencil_reach : stencil_reach + plane_count]
    laplace = 3.0 * stencil_weights[0] * centre
    for offset in range(1, stencil_reach + 1):
        upper = padded[:, stencil_reach + offset : stencil_reach + offset + plane_count]
        lower = padded[:, stencil_reach - offset : stencil_reach - offset + plane_count]
        across = jnp.roll(centre, offset, 2) + jnp.roll(centre, -offset, 2)
        along = jnp.roll(centre, offset, 3) + jnp.roll(centre, -offset, 3)
        laplace = laplace + stencil_weights[offset] * (upper + lower + across + along)
    return kinetic_factor * laplace + potential[None] * centre


def extend_planes(field):
    return padded_2(field, (("space", 1),), stencil_reach)


def chebyshev(filter_input, potential):
    applied = hamiltonian(extend_planes(filter_input), potential)
    inner_term = (applied - centre_value * filter_input) / half_width
    second = hamiltonian(extend_planes(inner_term), potential)
    return 2.0 * (second - centre_value * inner_term) / half_width - filter_input


def shards(panels, potential, block_index):
    block_rows = lax.dynamic_index_in_dim(panels, block_index[0], 0, keepdims=False)
    own_rows = chebyshev(block_rows, potential)
    cell_count = lax.axis_size("space") * potential.size
    panel_count = panels.shape[0]
    whole_block = lax.all_gather(own_rows, "band", axis=0, tiled=True)
    flat_block = whole_block.reshape(whole_block.shape[0], -1)
    flat_panels = panels.reshape(panel_count, panels.shape[1], -1)
    partial_gram = jnp.einsum(
        "prc,bc->prb",
        flat_panels,
        flat_block,
        precision=lax.Precision.HIGHEST,
        preferred_element_type=jnp.float32,
    )
    correlation = lax.psum(partial_gram, "space") / cell_count
    updated = (
        flat_panels
        - jnp.einsum(
            "prb,bc->prc",
            correlation,
            flat_block,
            precision=lax.Precision.HIGHEST,
            preferred_element_type=jnp.float32,
        )
    ).reshape(panels.shape)
    return (own_rows, updated)


def solution(mesh):
    return jax.shard_map(
        shards,
        mesh=mesh,
        in_specs=(P(None, "band", "space", None, None), P("space", None, None), P()),
        out_specs=(P("band", "space", None, None), P(None, "band", "space", None, None)),
        check_vma=False,
    )
```

profile of v0, /device:TPU:16, one launch (start us, length us, event | category | flops | bytes accessed | tf_op | source)
XLA Modules:
  0.0 974.4 jit_solution(7409465829039446807)
XLA Ops:
  7.2 0.0 all-gather.2.cloned.1.call-start
  7.9 1.3 dynamic-slice_bitcast_fusion
  9.2 0.2 fusion.146
  9.3 0.1 collective-permute-start
  9.4 0.5 collective-permute-start.1
  9.9 0.6 fusion.130
  10.6 1.7 fusion.136
  12.3 1.5 fusion.148
  13.8 1.5 fusion.135
  15.3 1.7 fusion.145
  17.0 1.8 fusion.141
  18.8 1.7 fusion.133
  20.5 1.7 fusion.132
  22.2 1.7 fusion.140
  23.9 1.7 fusion.144
  25.7 1.6 fusion.131
  27.2 1.5 fusion.139
  28.7 1.8 fusion.129
  30.4 1.7 fusion.128
  32.1 1.7 fusion.149
  33.8 1.5 fusion.127
  35.3 1.6 fusion.143
  36.8 0.8 broadcast_multiply_fusion.1
  37.7 0.6 fusion.126
  38.3 1.7 fusion.137
  39.9 1.7 fusion.150
  41.6 0.9 copy-done.3
  42.5 0.3 copy-done.4
  42.8 19.2 %broadcast_multiply_fusion = (f32[2,8,128,128]{3,2,1,0:T(8,128)S(1)}, f32[2,8,128,128]{3,2,1,0:T(8,128)S(1)}) fusion(f32[2,8,128,128]{3,2,1,0:T(8,128)S(1)} %dynamic-slice_bitcast_fusion, f32[8,128,128]{2,1,0:T(8,128)} %param.4, f32[2,8,128,6]{3,2,1,0:T(8,128)} %get-tuple-element.103, f32[2,8,128,122]{3,2,1,0:T(8,128)} %get-tuple-element.105, ...), kind=kLoop, calls=%fused_computation.163 | loop fusion | flops 22282240 | bytes 30408704 | tf_op jit(solution)/shard_map/div | solution.py:53
  62.0 0.6 fusion.120
  62.7 0.2 fusion.125
  62.9 1.2 fusion.107
  64.1 1.5 fusion.115
  65.7 1.8 fusion.106
  67.4 1.7 fusion.110
  69.1 1.6 fusion.118
  70.8 1.8 fusion.117
  72.5 1.7 fusion.109
  74.2 1.7 fusion.105
  75.9 1.5 fusion.119
  77.4 1.5 fusion.103
  78.9 1.7 fusion.122
  80.6 1.6 fusion.121
  82.2 1.5 fusion.111
  83.7 1.7 fusion.101
  85.4 1.5 fusion.123
  86.8 1.7 fusion.114
  88.5 2.8 collective-permute-start.2
  91.4 0.6 fusion.124
  92.0 1.6 fusion.113
  93.6 1.7 fusion.102
  95.3 11.6 %collective-permute-done.2 = f32[2,6,128,128]{3,2,1,0:T(8,128)S(1)} collective-permute-done((f32[2,6,128,128]{3,2,1,0:T(8,128)S(1)}, f32[2,6,128,128]{3,2,1,0:T(8,128)S(1)}, u32[]{:S(2)}, u32[]{:S(2)}) %collective-permute-start.2) | collective-permute-done | bytes 786464 | tf_op jit(solution)/shard_map/ppermute | solution.py:29
  106.9 5.7 collective-permute-done.3
  112.6 0.9 copy-done.6
  113.6 31.8 %fusion.20 = f32[2,8,128,128]{3,2,1,0:T(8,128)} fusion(f32[2,8,128,128]{3,2,1,0:T(8,128)S(1)} %get-tuple-element.4, f32[2,6,128,128]{3,2,1,0:T(8,128)} %copy-done.6, f32[2,6,128,128]{3,2,1,0:T(8,128)} %copy-done.5, f32[2,8,127,128]{3,2,1,0:T(8,128)} %get-tuple-element.51, f32[2,8,1,128]{3,2,1,0:T(1,128)} %get-tuple-element.53, ...), kind=kLoop, calls=%fused_computation.57 | loop fusion | flops 22544384 | bytes 31457284 | tf_op jit(solution)/shard_map/sub | solution.py:55
  145.3 0.0 all-gather.2.cloned.1.call-update
  145.4 5.3 reshape.14
  150.7 706.2 %all-gather.2.cloned.1.call-done = f32[64,8,128,128]{3,2,1,0:T(8,128)} async-done(((f32[2,8,128,128]{3,2,1,0:T(8,128)}), f32[64,8,128,128]{3,2,1,0:T(8,128)}) %all-gather.2.cloned.1.call-update) | async-done | bytes 33554448 | tf_op jit(solution)/shard_map/all_gather | solution.py:63
  856.9 50.0 %fusion.4 = f32[3,2,64]{2,0,1:T(4,128)S(1)} fusion(f32[3,2,8,128,128]{4,3,2,1,0:T(8,128)S(1)} %copy-done, f32[64,8,128,128]{3,2,1,0:T(8,128)} %all-gather.2.cloned.1.call-done), kind=kOutput, calls=%fused_computation.45 | convolution fusion | flops 603979776 | bytes 36701696 | tf_op jit(solution)/shard_map/prc,bc->prb/dot_general | solution.py:66
  906.9 7.5 psum.7
  914.4 24.4 %reshape.19 = f32[64,131072,1]{1,0,2:T(8,128)} reshape(f32[64,8,128,128]{3,2,1,0:T(8,128)} %all-gather.2.cloned.1.call-done) | data formatting | bytes 67108864 | tf_op jit(solution)/shard_map/reshape | solution.py:64
  938.8 22.7 %convolution_subtract_fusion = f32[3,2,131072]{2,0,1:T(4,128)} fusion(f32[64,131072,1]{1,0,2:T(8,128)} %reshape.19, f32[3,2,131072]{2,1,0:T(2,128)S(1)} %copy-done.1, f32[3,2,64]{2,0,1:T(4,128)S(1)} %psum.7), kind=kOutput, calls=%fused_computation | convolution fusion | flops 604766592 | bytes 39847424 | tf_op jit(solution)/shard_map/prb,bc->prc/dot_general | solution.py:76
  961.5 4.0 reshape.21
  965.4 1.9 copy.14
  (22 shorter events, 0.1 us)
Async XLA Ops:
  7.2 849.7 %all-gather.2.cloned.1.call-start = ((), (), s32[]{:S(2)}) async-start(), calls=%async_computation | async-start | bytes 34603008 | tf_op jit(solution)/shard_map/all_gather | solution.py:63
  9.3 32.3 %collective-permute-start = (f32[2,6,128,128]{3,2,1,0:T(8,128)S(1)}, f32[2,6,128,128]{3,2,1,0:T(8,128)S(1)}, u32[]{:S(2)}, u32[]{:S(2)}) collective-permute-start(f32[2,6,128,128]{3,2,1,0:T(8,128)S(1)} %get-tuple-element.96), channel_id=1, source_target_pairs={{1,0},{2,1},{3,2},{0,3},{5,4},{6,5},{7,6},{4,7},{9,8},{10,9},{11,1... | collective-permute-start | bytes 2359304 | tf_op jit(solution)/shard_map/ppermute | solution.py:29
  9.4 32.2 %collective-permute-start.1 = (f32[2,6,128,128]{3,2,1,0:T(8,128)S(1)}, f32[2,6,128,128]{3,2,1,0:T(8,128)S(1)}, u32[]{:S(2)}, u32[]{:S(2)}) collective-permute-start(f32[2,6,128,128]{3,2,1,0:T(8,128)S(1)} %get-tuple-element.97), channel_id=1, source_target_pairs={{0,1},{1,2},{2,3},{3,0},{4,5},{5,6},{6,7},{7,4},{8,9},{9,10},{10,1... | collective-permute-start | bytes 2359304 | tf_op jit(solution)/shard_map/ppermute | solution.py:28
  35.3 1.6 copy-start.2
  41.6 0.9 copy-start.3
  41.6 1.2 copy-start.4
  88.5 18.4 %collective-permute-start.2 = (f32[2,6,128,128]{3,2,1,0:T(8,128)S(1)}, f32[2,6,128,128]{3,2,1,0:T(8,128)S(1)}, u32[]{:S(2)}, u32[]{:S(2)}) collective-permute-start(f32[2,6,128,128]{3,2,1,0:T(8,128)S(1)} %get-tuple-element.54), channel_id=1, source_target_pairs={{1,0},{2,1},{3,2},{0,3},{5,4},{6,5},{7,6},{4,7},{9,8},{10,9},{11,1... | collective-permute-start | bytes 2359304 | tf_op jit(solution)/shard_map/ppermute | solution.py:29
  91.4 21.3 %collective-permute-start.3 = (f32[2,6,128,128]{3,2,1,0:T(8,128)S(1)}, f32[2,6,128,128]{3,2,1,0:T(8,128)S(1)}, u32[]{:S(2)}, u32[]{:S(2)}) collective-permute-start(f32[2,6,128,128]{3,2,1,0:T(8,128)S(1)} %get-tuple-element.55), channel_id=1, source_target_pairs={{0,1},{1,2},{2,3},{3,0},{4,5},{5,6},{6,7},{7,4},{8,9},{9,10},{10,1... | collective-permute-start | bytes 2359304 | tf_op jit(solution)/shard_map/ppermute | solution.py:28
  106.9 5.7 copy-start.5
  112.6 0.9 copy-start.6
  145.3 711.5 %copy-start = (f32[3,2,8,128,128]{4,3,2,1,0:T(8,128)S(1)}, f32[3,2,8,128,128]{4,3,2,1,0:T(8,128)}, u32[]{:S(2)}) copy-start(f32[3,2,8,128,128]{4,3,2,1,0:T(8,128)} %param.3) | copy-start | bytes 9437188
  914.4 24.4 %copy-start.1 = (f32[3,2,131072]{2,1,0:T(2,128)S(1)}, f32[3,2,131072]{2,1,0:T(2,128)}, u32[]{:S(2)}) copy-start(f32[3,2,131072]{2,1,0:T(2,128)} %reshape.14) | copy-start | bytes 9437188
Sparse Core Ops, SparseCore 0:
  145.5 711.3 all-gather.1
where the time goes:
time: 990 us; the launch traced here: 974 us
  waiting for transfers between devices  724 us (73%)
  local copies, waits for them, and re-layouts  100 us (10%)
  matrix products  72.7 us (7%)
  other arithmetic  51.8 us (5%)
  between operations  15.1 us (2%)
    all_gather x1, waiting for transfers between devices, shards(): whole_block = lax.all_gather(own_rows, 'band', axis=0, tiled=True)  706 us
    dot_general x1, matrix products, shards(): jnp.einsum('prc,bc->prb', flat_panels, flat_block, precision=lax.Precisio...  50 us
    slice x24, local copies, waits for them, and re-layouts, hamiltonian(): along = jnp.roll(centre, offset, 3) + jnp.roll(centre, -offset, 3)  40.7 us
    sub x1, other arithmetic, chebyshev(): 2.0 * (second - centre_value * inner_term) / half_width - filter_input  31.8 us
    reshape x1, local copies, waits for them, and re-layouts, shards(): flat_block = whole_block.reshape(whole_block.shape[0], -1)  24.4 us
    dot_general x1, matrix products, shards(): jnp.einsum('prb,bc->prc', correlation, flat_block, precision=lax.Precisio...  22.7 us
    slice x24, local copies, waits for them, and re-layouts, hamiltonian(): across = jnp.roll(centre, offset, 2) + jnp.roll(centre, -offset, 2)  20.4 us
  transfers between devices with their start and end apart: 5, of which 3 were waited for; matrix products, arithmetic and copies ran while one was open for 4% of the time, Pallas kernels for 0%

commit v1 on v0

v1 whole, which is shorter than its diff:
```python
import jax
import jax.numpy as jnp
from jax import lax
from jax.experimental import pallas as pl
from jax.experimental.pallas import tpu as pltpu
from jax.sharding import PartitionSpec as P

stencil_weights = (
    -5369.0 / 1800.0,
    12.0 / 7.0,
    -15.0 / 56.0,
    10.0 / 189.0,
    -1.0 / 112.0,
    2.0 / 1925.0,
    -1.0 / 16632.0,
)
reach = 6
kinetic_factor = -0.5 / 0.25
centre_value = 32.25
half_width = 10.75
vmem_bytes = 48 * 1024 * 1024


def stencil_kernel(second, lo_ref, mid_ref, hi_ref, pot_ref, *rest):
    if second:
        before_ref, out_ref, pad_ref = rest
    else:
        out_ref, pad_ref = rest
    planes = mid_ref.shape[1]
    rows, columns = mid_ref.shape[2:]
    pad_ref[0:reach] = lo_ref[0]
    pad_ref[reach : reach + planes] = mid_ref[0]
    pad_ref[reach + planes : 2 * reach + planes] = hi_ref[0]

    def one_plane(z, carry):
        centre = pad_ref[z + reach]
        laplace = 3.0 * stencil_weights[0] * centre
        for k in range(1, reach + 1):
            total = pad_ref[z + reach + k] + pad_ref[z + reach - k]
            total = total + (pltpu.roll(centre, k, 0) + pltpu.roll(centre, rows - k, 0))
            total = total + (pltpu.roll(centre, k, 1) + pltpu.roll(centre, columns - k, 1))
            laplace = laplace + stencil_weights[k] * total
        applied = kinetic_factor * laplace + pot_ref[z] * centre
        term = (applied - centre_value * centre) * (1.0 / half_width)
        if second:
            term = 2.0 * term - before_ref[0, z]
        out_ref[0, z] = term
        return carry

    lax.fori_loop(0, planes, one_plane, 0)


def stencil(lo, mid, hi, potential, before=None):
    bands, planes, rows, columns = mid.shape

    def field(depth):
        return pl.BlockSpec((1, depth, rows, columns), lambda b: (b, 0, 0, 0))

    operands = [lo, mid, hi, potential] + ([] if before is None else [before])
    specs = [field(reach), field(planes), field(reach)]
    specs += [pl.BlockSpec((planes, rows, columns), lambda b: (0, 0, 0))]
    specs += [] if before is None else [field(planes)]

    def body(*refs):
        stencil_kernel(before is not None, *refs)

    return pl.pallas_call(
        body,
        grid=(bands,),
        in_specs=specs,
        out_specs=field(planes),
        out_shape=jax.ShapeDtypeStruct(mid.shape, jnp.float32),
        scratch_shapes=[pltpu.VMEM((planes + 2 * reach, rows, columns), jnp.float32)],
        compiler_params=pltpu.CompilerParams(vmem_limit_bytes=vmem_bytes),
        cost_estimate=pl.CostEstimate(flops=50 * mid.size, bytes_accessed=16 * mid.size, transcendentals=0),
        name="stencil",
    )(*operands)


def split(value):
    high = value.astype(jnp.bfloat16)
    low = (value - high.astype(jnp.float32)).astype(jnp.bfloat16)
    return high, low


def gram_kernel(panel_ref, block_ref, out_ref):
    segments = 32
    rows = panel_ref.shape[0] // segments
    bands = block_ref.shape[0] // segments
    half = segments // 2
    contract = (((1,), (1,)), ((), ()))

    def one(j, total):
        def pair(ref, count):
            first = ref[pl.ds(j, count, segments), :]
            other = ref[pl.ds(j + half, count, segments), :]
            return jnp.concatenate([first, other], axis=1)

        panel_high, panel_low = split(pair(panel_ref, rows))
        block_high, block_low = split(pair(block_ref, bands))
        both = jnp.concatenate([block_high, block_low], axis=0)
        wide = lax.dot_general(panel_high, both, contract, preferred_element_type=jnp.float32)
        narrow = lax.dot_general(panel_low, block_high, contract, preferred_element_type=jnp.float32)
        return total + (wide[:, :bands] + (wide[:, bands:] + narrow))

    out_ref[...] = lax.fori_loop(0, half, one, jnp.zeros((rows, bands), jnp.float32))


def gram(panel_rows, block_rows):
    rows, bands = panel_rows.shape[0] // 32, block_rows.shape[0] // 32
    return pl.pallas_call(
        gram_kernel,
        out_shape=jax.ShapeDtypeStruct((rows, bands), jnp.float32),
        compiler_params=pltpu.CompilerParams(vmem_limit_bytes=vmem_bytes),
        cost_estimate=pl.CostEstimate(
            flops=6 * rows * bands * 4096, bytes_accessed=4 * (panel_rows.size + block_rows.size), transcendentals=0
        ),
        name="gram",
    )(panel_rows, block_rows)


def update_kernel(corr_ref, block_ref, panel_ref, out_ref):
    segments = 32
    rows = panel_ref.shape[0] // segments
    bands = block_ref.shape[0] // segments
    half = segments // 2
    corr_high, corr_low = split(corr_ref[...])
    left = jnp.concatenate([corr_high, corr_high, corr_low], axis=1)

    def one(j, carry):
        pair = jnp.concatenate(
            [block_ref[pl.ds(j, bands, segments), :], block_ref[pl.ds(j + half, bands, segments), :]], axis=1
        )
        high, low = split(pair)
        product = jnp.dot(left, jnp.concatenate([high, low, high], axis=0), preferred_element_type=jnp.float32)
        for start, part in ((j, product[:, :128]), (j + half, product[:, 128:])):
            place = pl.ds(start, rows, segments)
            out_ref[place, :] = panel_ref[place, :] - part
        return carry

    lax.fori_loop(0, half, one, 0)


def update(correlation, block_rows, panel_rows):
    rows, bands = correlation.shape
    return pl.pallas_call(
        update_kernel,
        out_shape=jax.ShapeDtypeStruct(panel_rows.shape, jnp.float32),
        compiler_params=pltpu.CompilerParams(vmem_limit_bytes=vmem_bytes),
        cost_estimate=pl.CostEstimate(
            flops=6 * rows * bands * 4096, bytes_accessed=8 * panel_rows.size, transcendentals=0
        ),
        name="update",
    )(correlation, block_rows, panel_rows)


def halos(field):
    size, planes = lax.axis_size("space"), field.shape[1]
    up = [(i, (i + 1) % size) for i in range(size)]
    down = [(j, i) for i, j in up]
    before = lax.ppermute(field[:, planes - reach :], "space", up)
    after = lax.ppermute(field[:, :reach], "space", down)
    return before, after


def summed(value):
    size = lax.axis_size("space")
    parts = [value]
    for step in range(1, size):
        parts.append(lax.ppermute(value, "space", [(i, (i + step) % size) for i in range(size)]))
    value = sum(parts[1:], parts[0])
    bands = lax.axis_size("band")
    for stride, length in ((1, 2), (2, 4), (8, 4)):
        parts = [value]
        for step in range(1, length):
            moves = []
            for i in range(bands):
                digit = i // stride % length
                moves.append((i, i + ((digit + step) % length - digit) * stride))
            parts.append(lax.ppermute(value, "band", moves))
        value = sum(parts[1:], parts[0])
    return value


def shards(panels, potential, block_index):
    count, own = panels.shape[:2]
    bands = lax.axis_size("band")
    cell_count = lax.axis_size("space") * potential.size
    lanes = panels.shape[-1]
    chunked = panels.reshape(count * own, bands, -1, lanes)
    sent = jnp.swapaxes(chunked, 0, 1)
    panel_rows = lax.all_to_all(sent, "band", 0, 0, tiled=True).reshape(-1, lanes)

    block = lax.dynamic_index_in_dim(panels, block_index[0], 0, keepdims=False)
    before, after = halos(block)
    first = stencil(before, block, after, potential)
    before, after = halos(first)
    filtered = stencil(before, first, after, potential, block)

    own_chunks = jnp.swapaxes(filtered.reshape(own, bands, -1, lanes), 0, 1)
    block_rows = lax.all_to_all(own_chunks, "band", 0, 0, tiled=True).reshape(-1, lanes)

    partial = gram(panel_rows, block_rows)
    correlation = summed(partial) * (1.0 / cell_count)
    fresh = update(correlation, block_rows, panel_rows).reshape(sent.shape)
    home = lax.all_to_all(fresh, "band", 0, 0, tiled=True)
    updated = jnp.swapaxes(home, 0, 1).reshape(panels.shape)
    return filtered, updated


def solution(mesh):
    return jax.shard_map(
        shards,
        mesh=mesh,
        in_specs=(P(None, "band", "space", None, None), P("space", None, None), P()),
        out_specs=(P("band", "space", None, None), P(None, "band", "space", None, None)),
        check_vma=False,
    )
```

time: 990 us -> 214 us (0.22); the launches traced: 974 us -> 213 us
  waiting for transfers between devices: 724 us -> 78.7 us
  local copies, waits for them, and re-layouts: 100 us -> 9.92 us
  blocking collectives: 7.48 us -> 82.3 us
  matrix products: 72.7 us -> 0 us
  other arithmetic: 51.8 us -> 0.08 us
  Pallas kernels: 0 us -> 24.8 us
  between operations: 15.1 us -> 1.46 us
  starting transfers between devices: 3.43 us -> 15.7 us
    all_gather x1 -> x0, waiting for transfers between devices: 706 us -> none  [shards(): whole_block = lax.all_gather(own_rows, 'band', axis=0, tiled=True)]
    all_to_all x0 -> x2, blocking collectives: none -> 82.3 us  [the longest x1 43.1 us: shards(): lax.all_to_all(sent, 'band', 0, 0, tiled=True).reshape(-1, lanes)]
    dot_general x2 -> x0, matrix products: 72.7 us -> none  [the longest x1 50 us: shards(): jnp.einsum('prc,bc->prb', flat_panels, flat_block, precision=lax.Precisio...]
    slice x50 -> x2, local copies, waits for them, and re-layouts: 61.4 us -> 0.33 us  [halos(): after = lax.ppermute(field[:, :reach], 'space', down)]
    ppermute x4 -> x14, waiting for transfers between devices: 17.3 us -> 64.9 us  [the longest x2 29.7 us: halos(): after = lax.ppermute(field[:, :reach], 'space', down)]
    sub x1 -> x0, other arithmetic: 31.8 us -> none  [chebyshev(): 2.0 * (second - centre_value * inner_term) / half_width - filter_input]
    reshape x4 -> x2, local copies, waits for them, and re-layouts: 35.6 us -> 6.29 us  [the longest x1 4 us: shards(): chunked = panels.reshape(count * own, bands, -1, lanes)]
    pallas_call x0 -> x4, Pallas kernels: none -> 24.8 us  [the longest x2 10.4 us: stencil(): pl.pallas_call(body, grid=(bands,), in_specs=specs, out_specs=field(plane...]
  transfers between devices with their start and end apart: 5 -> 15, of which waited for: 3 -> 15; matrix products, arithmetic and copies ran while one was open for 4% -> 2% of each run, Pallas kernels for 0% -> 0%
where the time goes in v1:
time: 214 us; the launch traced here: 213 us
  blocking collectives  82.3 us (38%)
  waiting for transfers between devices  78.7 us (37%)
  Pallas kernels  24.8 us (12%)
  starting transfers between devices  15.7 us (7%)
  local copies, waits for them, and re-layouts  9.92 us (5%)
    all_to_all x1, blocking collectives, shards(): lax.all_to_all(sent, 'band', 0, 0, tiled=True).reshape(-1, lanes)  43.1 us
    all_to_all x1, blocking collectives, shards(): home = lax.all_to_all(fresh, 'band', 0, 0, tiled=True)  39.2 us
    ppermute x2, waiting for transfers between devices, halos(): after = lax.ppermute(field[:, :reach], 'space', down)  29.7 us
    ppermute x7, waiting for transfers between devices, summed(): parts.append(lax.ppermute(value, 'band', moves))  16 us
    all_to_all x1, waiting for transfers between devices, shards(): lax.all_to_all(own_chunks, 'band', 0, 0, tiled=True).reshape(-1, lanes)  13.8 us
    ppermute x2, waiting for transfers between devices, halos(): before = lax.ppermute(field[:, planes - reach:], 'space', up)  11.9 us
    pallas_call x2, Pallas kernels, stencil(): pl.pallas_call(body, grid=(bands,), in_specs=specs, out_specs=field(plane...  10.4 us
    all_to_all x1, starting transfers between devices, shards(): lax.all_to_all(own_chunks, 'band', 0, 0, tiled=True).reshape(-1, lanes)  8.63 us
  transfers between devices with their start and end apart: 15, of which 15 were waited for; matrix products, arithmetic and copies ran while one was open for 2% of the time, Pallas kernels for 0%

profile of v1, /device:TPU:16, one launch (start us, length us, event | category | flops | bytes accessed | tf_op | source)
XLA Modules:
  0.0 212.9 jit_solution(2659262109449965402)
XLA Ops:
  0.6 0.0 copy-start.1
  1.3 1.3 dynamic-slice_bitcast_fusion.refs_1_.refs_4_
  2.7 0.2 fusion.1
  2.8 0.1 collective-permute-start.1
  2.9 0.5 collective-permute-start
  3.4 15.0 %collective-permute-done.1.refs_2_ = f32[2,6,128,128]{3,2,1,0:T(8,128)S(1)} collective-permute-done((f32[2,6,128,128]{3,2,1,0:T(8,128)S(1)}, f32[2,6,128,128]{3,2,1,0:T(8,128)S(1)}, u32[]{:S(2)}, u32[]{:S(2)}) %collective-permute-start.1) | collective-permute-done | bytes 786464 | tf_op jit(solution)/shard_map/ppermute | solution.py:162
  18.4 5.9 %collective-permute-done.refs_0_ = f32[2,6,128,128]{3,2,1,0:T(8,128)S(1)} collective-permute-done((f32[2,6,128,128]{3,2,1,0:T(8,128)S(1)}, f32[2,6,128,128]{3,2,1,0:T(8,128)S(1)}, u32[]{:S(2)}, u32[]{:S(2)}) %collective-permute-start) | collective-permute-done | bytes 786464 | tf_op jit(solution)/shard_map/ppermute | solution.py:161
  24.3 0.0 copy-done.1
  24.3 4.8 %stencil.2.refs_1_ = f32[2,8,128,128]{3,2,1,0:T(8,128)S(1)} custom-call(f32[2,6,128,128]{3,2,1,0:T(8,128)S(1)} %collective-permute-done.refs_0_, f32[2,8,128,128]{3,2,1,0:T(8,128)S(1)} %dynamic-slice_bitcast_fusion.refs_1_.refs_4_, f32[2,6,128,128]{3,2,1,0:T(8,128)S(1)} %collective-permute-done.1.refs_2_, f32[8,128,128]{2,1,0:T(8,128)S(1)} %copy-done.1), custom_call_target="tpu_custom_call" | custom-call | flops 13107200 | bytes 4194304 | tf_op jit(solution)/shard_map/stencil/pallas_call | solution.py:67
  29.1 0.2 fusion
  29.2 0.1 collective-permute-start.3
  29.3 0.5 collective-permute-start.2
  29.8 14.8 %collective-permute-done.3.refs_2_ = f32[2,6,128,128]{3,2,1,0:T(8,128)S(1)} collective-permute-done((f32[2,6,128,128]{3,2,1,0:T(8,128)S(1)}, f32[2,6,128,128]{3,2,1,0:T(8,128)S(1)}, u32[]{:S(2)}, u32[]{:S(2)}) %collective-permute-start.3) | collective-permute-done | bytes 786464 | tf_op jit(solution)/shard_map/ppermute | solution.py:162
  44.6 6.0 %collective-permute-done.2.refs_0_ = f32[2,6,128,128]{3,2,1,0:T(8,128)S(1)} collective-permute-done((f32[2,6,128,128]{3,2,1,0:T(8,128)S(1)}, f32[2,6,128,128]{3,2,1,0:T(8,128)S(1)}, u32[]{:S(2)}, u32[]{:S(2)}) %collective-permute-start.2) | collective-permute-done | bytes 786464 | tf_op jit(solution)/shard_map/ppermute | solution.py:161
  50.6 5.6 %stencil.3 = f32[2,8,128,128]{3,2,1,0:T(8,128)} custom-call(f32[2,6,128,128]{3,2,1,0:T(8,128)S(1)} %collective-permute-done.2.refs_0_, f32[2,8,128,128]{3,2,1,0:T(8,128)S(1)} %stencil.2.refs_1_, f32[2,6,128,128]{3,2,1,0:T(8,128)S(1)} %collective-permute-done.3.refs_2_, f32[8,128,128]{2,1,0:T(8,128)S(1)} %copy-done.1, ...), custom_call_target="tpu_custom_call" | custom-call | flops 13107200 | bytes 4194304 | tf_op jit(solution)/shard_map/stencil/pallas_call | solution.py:67
  56.2 2.3 %copy.11 = f32[2,32,32,128]{3,2,0,1:T(8,128)} copy(f32[2,32,32,128]{3,2,1,0:T(8,128)} %bitcast.27) | data formatting | bytes 2097152 | tf_op jit(solution)/shard_map/reshape | solution.py:200
  58.5 8.6 %all-to-all-start.1 = ((f32[32,2,32,128]{3,2,1,0:T(8,128)}), f32[32,2,32,128]{3,2,1,0:T(8,128)S(1)}, u32[]{:S(2)}, u32[]{:S(2)}) async-start(f32[32,2,32,128]{3,2,1,0:T(8,128)} %bitcast.15), calls=%async_computation.1 | async-start | bytes 2097152 | tf_op jit(solution)/shard_map/all_to_all | solution.py:201
  67.1 4.0 %copy.10 = f32[6,32,32,128]{3,2,0,1:T(8,128)} copy(f32[6,32,32,128]{3,2,1,0:T(8,128)} %bitcast.26) | data formatting | bytes 6291456 | tf_op jit(solution)/shard_map/reshape | solution.py:190
  71.1 13.8 %all-to-all-done.1 = f32[32,2,32,128]{3,2,1,0:T(8,128)S(1)} async-done(((f32[32,2,32,128]{3,2,1,0:T(8,128)}), f32[32,2,32,128]{3,2,1,0:T(8,128)S(1)}, u32[]{:S(2)}, u32[]{:S(2)}) %all-to-all-start.1) | async-done | bytes 1048608 | tf_op jit(solution)/shard_map/all_to_all | solution.py:201
  84.9 43.1 %all_to_all.15 = f32[32,6,32,128]{3,2,1,0:T(8,128)S(1)} all-to-all(f32[32,6,32,128]{3,2,1,0:T(8,128)} %bitcast.24), channel_id=1, replica_groups=mesh['band'=32,'space'=4] {'band'}, dimensions={0} | all-to-all | bytes 6291456 | tf_op jit(solution)/shard_map/all_to_all | solution.py:192
  128.1 0.0 copy-start
  128.1 6.5 %gram.1 = f32[192,64]{1,0:T(8,128)S(1)} custom-call(f32[6144,128]{1,0:T(8,128)S(1)} %bitcast.19, f32[2048,128]{1,0:T(8,128)S(1)} %bitcast.22), custom_call_target="tpu_custom_call" | custom-call | flops 301989888 | bytes 4194304 | tf_op jit(solution)/shard_map/gram/pallas_call | solution.py:111
  134.5 0.1 collective-permute-start.6
  134.6 0.3 collective-permute-start.5
  134.9 0.2 collective-permute-start.4
  135.1 2.5 %collective-permute-done.6 = f32[192,64]{1,0:T(8,128)S(1)} collective-permute-done((f32[192,64]{1,0:T(8,128)S(1)}, f32[192,64]{1,0:T(8,128)S(1)}, u32[]{:S(2)}, u32[]{:S(2)}) %collective-permute-start.6) | collective-permute-done | bytes 49184 | tf_op jit(solution)/shard_map/ppermute | solution.py:170
  137.6 4.2 %collective-permute-done.5 = f32[192,64]{1,0:T(8,128)S(1)} collective-permute-done((f32[192,64]{1,0:T(8,128)S(1)}, f32[192,64]{1,0:T(8,128)S(1)}, u32[]{:S(2)}, u32[]{:S(2)}) %collective-permute-start.5) | collective-permute-done | bytes 49184 | tf_op jit(solution)/shard_map/ppermute | solution.py:170
  141.8 0.6 collective-permute-done.4
  142.4 0.4 collective-permute-start.7
  142.8 4.3 %collective-permute-done.7 = f32[192,64]{1,0:T(8,128)S(1)} collective-permute-done((f32[192,64]{1,0:T(8,128)S(1)}, f32[192,64]{1,0:T(8,128)S(1)}, u32[]{:S(2)}, u32[]{:S(2)}) %collective-permute-start.7) | collective-permute-done | bytes 49184 | tf_op jit(solution)/shard_map/ppermute | solution.py:180
  147.1 0.3 collective-permute-start.10
  147.4 2.4 %collective-permute-start.9 = (f32[192,64]{1,0:T(8,128)S(1)}, f32[192,64]{1,0:T(8,128)S(1)}, u32[]{:S(2)}, u32[]{:S(2)}) collective-permute-start(f32[192,64]{1,0:T(8,128)S(1)} %add.38), channel_id=1, source_target_pairs={{0,16},{4,20},{8,24},{12,28},{16,0},{20,4},{24,8},{28,12},{32,48},... | collective-permute-start | bytes 147464 | tf_op jit(solution)/shard_map/ppermute | solution.py:180
  149.8 0.0 collective-permute-start.8
  149.8 2.0 collective-permute-done.10
  151.8 1.7 collective-permute-done.9
  153.5 2.1 collective-permute-done.8
  155.7 0.9 collective-permute-start.13
  156.6 0.9 collective-permute-start.12
  157.5 0.4 collective-permute-start.11
  158.0 2.4 %collective-permute-done.13 = f32[192,64]{1,0:T(8,128)S(1)} collective-permute-done((f32[192,64]{1,0:T(8,128)S(1)}, f32[192,64]{1,0:T(8,128)S(1)}, u32[]{:S(2)}, u32[]{:S(2)}) %collective-permute-start.13) | collective-permute-done | bytes 49184 | tf_op jit(solution)/shard_map/ppermute | solution.py:180
  160.4 2.4 %collective-permute-done.12 = f32[192,64]{1,0:T(8,128)S(1)} collective-permute-done((f32[192,64]{1,0:T(8,128)S(1)}, f32[192,64]{1,0:T(8,128)S(1)}, u32[]{:S(2)}, u32[]{:S(2)}) %collective-permute-start.12) | collective-permute-done | bytes 49184 | tf_op jit(solution)/shard_map/ppermute | solution.py:180
  162.8 1.0 collective-permute-done.11
  163.8 0.0 copy-done
  163.8 8.0 %update.1 = f32[6144,128]{1,0:T(8,128)S(1)} custom-call(f32[192,64]{1,0:T(8,128)S(1)} %add_multiply_fusion.corr_ref, f32[2048,128]{1,0:T(8,128)S(1)} %bitcast.23, f32[6144,128]{1,0:T(8,128)} %bitcast.20), custom_call_target="tpu_custom_call" | custom-call | flops 301989888 | bytes 6291456 | tf_op jit(solution)/shard_map/update/pallas_call | solution.py:146
  171.8 39.2 %all_to_all.16 = f32[32,6,32,128]{3,2,1,0:T(8,128)S(1)} all-to-all(f32[32,6,32,128]{3,2,1,0:T(8,128)S(1)} %bitcast.21), channel_id=1, replica_groups=mesh['band'=32,'space'=4] {'band'}, dimensions={0} | all-to-all | bytes 6291456 | tf_op jit(solution)/shard_map/all_to_all | solution.py:206
  211.0 2.0 copy.7
  (4 shorter events, 0.1 us)
Async XLA Ops:
  0.6 23.6 %copy-start.1 = (f32[8,128,128]{2,1,0:T(8,128)S(1)}, f32[8,128,128]{2,1,0:T(8,128)}, u32[]{:S(2)}) copy-start(f32[8,128,128]{2,1,0:T(8,128)} %refs_3_.3) | copy-start | bytes 1572868
  2.8 15.6 %collective-permute-start.1 = (f32[2,6,128,128]{3,2,1,0:T(8,128)S(1)}, f32[2,6,128,128]{3,2,1,0:T(8,128)S(1)}, u32[]{:S(2)}, u32[]{:S(2)}) collective-permute-start(f32[2,6,128,128]{3,2,1,0:T(8,128)S(1)} %get-tuple-element.4), channel_id=1, source_target_pairs={{1,0},{2,1},{3,2},{0,3},{5,4},{6,5},{7,6},{4,7},{9,8},{10,9},{11,1... | collective-permute-start | bytes 2359304 | tf_op jit(solution)/shard_map/ppermute | solution.py:162
  2.9 21.3 %collective-permute-start = (f32[2,6,128,128]{3,2,1,0:T(8,128)S(1)}, f32[2,6,128,128]{3,2,1,0:T(8,128)S(1)}, u32[]{:S(2)}, u32[]{:S(2)}) collective-permute-start(f32[2,6,128,128]{3,2,1,0:T(8,128)S(1)} %get-tuple-element.5), channel_id=1, source_target_pairs={{0,1},{1,2},{2,3},{3,0},{4,5},{5,6},{6,7},{7,4},{8,9},{9,10},{10,1... | collective-permute-start | bytes 2359304 | tf_op jit(solution)/shard_map/ppermute | solution.py:161
  29.2 15.3 %collective-permute-start.3 = (f32[2,6,128,128]{3,2,1,0:T(8,128)S(1)}, f32[2,6,128,128]{3,2,1,0:T(8,128)S(1)}, u32[]{:S(2)}, u32[]{:S(2)}) collective-permute-start(f32[2,6,128,128]{3,2,1,0:T(8,128)S(1)} %get-tuple-element.2), channel_id=1, source_target_pairs={{1,0},{2,1},{3,2},{0,3},{5,4},{6,5},{7,6},{4,7},{9,8},{10,9},{11,1... | collective-permute-start | bytes 2359304 | tf_op jit(solution)/shard_map/ppermute | solution.py:162
  29.3 21.3 %collective-permute-start.2 = (f32[2,6,128,128]{3,2,1,0:T(8,128)S(1)}, f32[2,6,128,128]{3,2,1,0:T(8,128)S(1)}, u32[]{:S(2)}, u32[]{:S(2)}) collective-permute-start(f32[2,6,128,128]{3,2,1,0:T(8,128)S(1)} %get-tuple-element.3), channel_id=1, source_target_pairs={{0,1},{1,2},{2,3},{3,0},{4,5},{5,6},{6,7},{7,4},{8,9},{9,10},{10,1... | collective-permute-start | bytes 2359304 | tf_op jit(solution)/shard_map/ppermute | solution.py:161
  58.5 26.4 %all-to-all-start.1 = ((f32[32,2,32,128]{3,2,1,0:T(8,128)}), f32[32,2,32,128]{3,2,1,0:T(8,128)S(1)}, u32[]{:S(2)}, u32[]{:S(2)}) async-start(f32[32,2,32,128]{3,2,1,0:T(8,128)} %bitcast.15), calls=%async_computation.1 | async-start | bytes 2097152 | tf_op jit(solution)/shard_map/all_to_all | solution.py:201
  128.1 35.7 %copy-start = (f32[32,6,32,128]{3,2,1,0:T(8,128)}, f32[32,6,32,128]{3,2,1,0:T(8,128)S(1)}, u32[]{:S(2)}) copy-start(f32[32,6,32,128]{3,2,1,0:T(8,128)S(1)} %all_to_all.15) | copy-start | bytes 9437188
  134.5 3.1 %collective-permute-start.6 = (f32[192,64]{1,0:T(8,128)S(1)}, f32[192,64]{1,0:T(8,128)S(1)}, u32[]{:S(2)}, u32[]{:S(2)}) collective-permute-start(f32[192,64]{1,0:T(8,128)S(1)} %gram.1), channel_id=1, source_target_pairs={{0,3},{1,0},{2,1},{3,2},{4,7},{5,4},{6,5},{7,6},{8,11},{9,8},{10,9... | collective-permute-start | bytes 147464 | tf_op jit(solution)/shard_map/ppermute | solution.py:170
  134.6 7.2 %collective-permute-start.5 = (f32[192,64]{1,0:T(8,128)S(1)}, f32[192,64]{1,0:T(8,128)S(1)}, u32[]{:S(2)}, u32[]{:S(2)}) collective-permute-start(f32[192,64]{1,0:T(8,128)S(1)} %gram.1), channel_id=1, source_target_pairs={{0,2},{1,3},{2,0},{3,1},{4,6},{5,7},{6,4},{7,5},{8,10},{9,11},{10,... | collective-permute-start | bytes 147464 | tf_op jit(solution)/shard_map/ppermute | solution.py:170
  134.9 7.4 %collective-permute-start.4 = (f32[192,64]{1,0:T(8,128)S(1)}, f32[192,64]{1,0:T(8,128)S(1)}, u32[]{:S(2)}, u32[]{:S(2)}) collective-permute-start(f32[192,64]{1,0:T(8,128)S(1)} %gram.1), channel_id=1, source_target_pairs={{0,1},{1,2},{2,3},{3,0},{4,5},{5,6},{6,7},{7,4},{8,9},{9,10},{10,1... | collective-permute-start | bytes 147464 | tf_op jit(solution)/shard_map/ppermute | solution.py:170
  142.4 4.7 %collective-permute-start.7 = (f32[192,64]{1,0:T(8,128)S(1)}, f32[192,64]{1,0:T(8,128)S(1)}, u32[]{:S(2)}, u32[]{:S(2)}) collective-permute-start(f32[192,64]{1,0:T(8,128)S(1)} %add_add_fusion.1), channel_id=1, source_target_pairs={{0,4},{4,0},{8,12},{12,8},{16,20},{20,16},{24,28},{28,24},{32,36},... | collective-permute-start | bytes 147464 | tf_op jit(solution)/shard_map/ppermute | solution.py:180
  147.1 4.7 %collective-permute-start.10 = (f32[192,64]{1,0:T(8,128)S(1)}, f32[192,64]{1,0:T(8,128)S(1)}, u32[]{:S(2)}, u32[]{:S(2)}) collective-permute-start(f32[192,64]{1,0:T(8,128)S(1)} %add.38), channel_id=1, source_target_pairs={{0,24},{4,28},{8,0},{12,4},{16,8},{20,12},{24,16},{28,20},{32,56},... | collective-permute-start | bytes 147464 | tf_op jit(solution)/shard_map/ppermute | solution.py:180
  147.4 6.1 %collective-permute-start.9 = (f32[192,64]{1,0:T(8,128)S(1)}, f32[192,64]{1,0:T(8,128)S(1)}, u32[]{:S(2)}, u32[]{:S(2)}) collective-permute-start(f32[192,64]{1,0:T(8,128)S(1)} %add.38), channel_id=1, source_target_pairs={{0,16},{4,20},{8,24},{12,28},{16,0},{20,4},{24,8},{28,12},{32,48},... | collective-permute-start | bytes 147464 | tf_op jit(solution)/shard_map/ppermute | solution.py:180
  149.8 5.8 %collective-permute-start.8 = (f32[192,64]{1,0:T(8,128)S(1)}, f32[192,64]{1,0:T(8,128)S(1)}, u32[]{:S(2)}, u32[]{:S(2)}) collective-permute-start(f32[192,64]{1,0:T(8,128)S(1)} %add.38), channel_id=1, source_target_pairs={{0,8},{4,12},{8,16},{12,20},{16,24},{20,28},{24,0},{28,4},{32,40},... | collective-permute-start | bytes 147464 | tf_op jit(solution)/shard_map/ppermute | solution.py:180
  155.7 4.7 %collective-permute-start.13 = (f32[192,64]{1,0:T(8,128)S(1)}, f32[192,64]{1,0:T(8,128)S(1)}, u32[]{:S(2)}, u32[]{:S(2)}) collective-permute-start(f32[192,64]{1,0:T(8,128)S(1)} %add_add_fusion), channel_id=1, source_target_pairs={{0,96},{4,100},{8,104},{12,108},{16,112},{20,116},{24,120},{28,124... | collective-permute-start | bytes 147464 | tf_op jit(solution)/shard_map/ppermute | solution.py:180
  156.6 6.2 %collective-permute-start.12 = (f32[192,64]{1,0:T(8,128)S(1)}, f32[192,64]{1,0:T(8,128)S(1)}, u32[]{:S(2)}, u32[]{:S(2)}) collective-permute-start(f32[192,64]{1,0:T(8,128)S(1)} %add_add_fusion), channel_id=1, source_target_pairs={{0,64},{4,68},{8,72},{12,76},{16,80},{20,84},{24,88},{28,92},{32,9... | collective-permute-start | bytes 147464 | tf_op jit(solution)/shard_map/ppermute | solution.py:180
  157.5 6.2 %collective-permute-start.11 = (f32[192,64]{1,0:T(8,128)S(1)}, f32[192,64]{1,0:T(8,128)S(1)}, u32[]{:S(2)}, u32[]{:S(2)}) collective-permute-start(f32[192,64]{1,0:T(8,128)S(1)} %add_add_fusion), channel_id=1, source_target_pairs={{0,32},{4,36},{8,40},{12,44},{16,48},{20,52},{24,56},{28,60},{32,6... | collective-permute-start | bytes 147464 | tf_op jit(solution)/shard_map/ppermute | solution.py:180

commit v2 on v1

v2 whole, which is shorter than its diff:
```python
import jax
import jax.numpy as jnp
from jax import lax
from jax.experimental import pallas as pl
from jax.experimental.pallas import tpu as pltpu
from jax.sharding import Mesh, PartitionSpec as P

stencil_weights = (
    -5369.0 / 1800.0,
    12.0 / 7.0,
    -15.0 / 56.0,
    10.0 / 189.0,
    -1.0 / 112.0,
    2.0 / 1925.0,
    -1.0 / 16632.0,
)
reach = 6
kinetic_factor = -0.5 / 0.25
centre_value = 32.25
half_width = 10.75
vmem_bytes = 48 * 1024 * 1024


def stencil_kernel(second, lo_ref, mid_ref, hi_ref, pot_ref, *rest):
    if second:
        before_ref, out_ref, chunk_ref, pad_ref = rest
    else:
        out_ref, pad_ref = rest
    planes, rows, columns = mid_ref.shape[1:]
    pad_ref[0:reach] = lo_ref[0]
    pad_ref[reach : reach + planes] = mid_ref[0]
    pad_ref[reach + planes : 2 * reach + planes] = hi_ref[0]

    def one_plane(z, carry):
        centre = pad_ref[z + reach]
        laplace = 3.0 * stencil_weights[0] * centre
        for k in range(1, reach + 1):
            total = pad_ref[z + reach + k] + pad_ref[z + reach - k]
            total = total + (pltpu.roll(centre, k, 0) + pltpu.roll(centre, rows - k, 0))
            total = total + (pltpu.roll(centre, k, 1) + pltpu.roll(centre, columns - k, 1))
            laplace = laplace + stencil_weights[k] * total
        applied = kinetic_factor * laplace + pot_ref[z] * centre
        term = (applied - centre_value * centre) * (1.0 / half_width)
        if second:
            term = 2.0 * term - before_ref[0, z]
            cuts, copies, _, height, _ = chunk_ref.shape
            for i in range(cuts // planes):
                for j in range(copies):
                    chunk_ref[z * (cuts // planes) + i, j, 0] = term[i * height : (i + 1) * height]
        out_ref[0, z] = term
        return carry

    lax.fori_loop(0, planes, one_plane, 0)


def stencil(lo, mid, hi, potential, before=None, chunks=None):
    bands, planes, rows, columns = mid.shape

    def field(depth):
        return pl.BlockSpec((1, depth, rows, columns), lambda b: (b, 0, 0, 0))

    second = before is not None
    weight = 50 if second else 5000000
    operands = [lo, mid, hi, potential]
    specs = [field(reach), field(planes), field(reach)]
    specs += [pl.BlockSpec((planes, rows, columns), lambda b: (0, 0, 0))]
    out_specs, out_shape = [field(planes)], [jax.ShapeDtypeStruct(mid.shape, jnp.float32)]
    if second:
        operands.append(before)
        specs.append(field(planes))
        spots, copies = chunks
        height = planes * rows // spots
        out_specs.append(pl.BlockSpec((spots, copies, 1, height, columns), lambda b: (0, 0, b, 0, 0)))
        out_shape.append(jax.ShapeDtypeStruct((spots, copies, bands, height, columns), jnp.float32))

    def body(*refs):
        stencil_kernel(second, *refs)

    return pl.pallas_call(
        body,
        grid=(bands,),
        in_specs=specs,
        out_specs=out_specs,
        out_shape=out_shape,
        scratch_shapes=[pltpu.VMEM((planes + 2 * reach, rows, columns), jnp.float32)],
        compiler_params=pltpu.CompilerParams(vmem_limit_bytes=vmem_bytes),
        cost_estimate=pl.CostEstimate(flops=weight * mid.size, bytes_accessed=16 * mid.size, transcendentals=0),
        name="stencil",
    )(*operands)


def split(value):
    high = value.astype(jnp.bfloat16)
    low = (value - high.astype(jnp.float32)).astype(jnp.bfloat16)
    return high, low


def pair(ref, j):
    rows, segments = ref.shape[:2]
    flat = ref.reshape(rows * segments, ref.shape[2])
    first = flat[pl.ds(j, rows, segments), :]
    other = flat[pl.ds(j + segments // 2, rows, segments), :]
    return jnp.concatenate([first, other], axis=1)


def gram_kernel(panel_ref, block_ref, out_ref):
    rows, segments = panel_ref.shape[:2]
    bands = block_ref.shape[0]
    contract = (((1,), (1,)), ((), ()))

    def one(j, total):
        panel_high, panel_low = split(pair(panel_ref, j))
        block_high, block_low = split(pair(block_ref, j))
        both = jnp.concatenate([block_high, block_low], axis=0)
        wide = lax.dot_general(both, panel_high, contract, preferred_element_type=jnp.float32)
        narrow = lax.dot_general(block_high, panel_low, contract, preferred_element_type=jnp.float32)
        return total + (wide[:bands] + (wide[bands:] + narrow))

    out_ref[...] = lax.fori_loop(0, segments // 2, one, jnp.zeros((bands, rows), jnp.float32), unroll=4)


def gram(panel_rows, block_rows):
    rows, bands = panel_rows.shape[0], block_rows.shape[0]
    return pl.pallas_call(
        gram_kernel,
        out_shape=jax.ShapeDtypeStruct((bands, rows), jnp.float32),
        compiler_params=pltpu.CompilerParams(vmem_limit_bytes=vmem_bytes),
        cost_estimate=pl.CostEstimate(
            flops=6 * bands * panel_rows.size, bytes_accessed=4 * (panel_rows.size + block_rows.size), transcendentals=0
        ),
        name="gram",
    )(panel_rows, block_rows)


def update_kernel(scale, sums_ref, block_ref, panel_ref, out_ref):
    rows, segments, lanes = panel_ref.shape
    total = sums_ref[0]
    for i in range(1, sums_ref.shape[0]):
        total = total + sums_ref[i]
    corr_high, corr_low = split((total * scale).T)
    left = jnp.concatenate([corr_high, corr_high, corr_low], axis=1)
    flat_panel = panel_ref.reshape(rows * segments, lanes)
    flat_out = out_ref.reshape(rows * segments, lanes)
    half = segments // 2

    def one(j, carry):
        high, low = split(pair(block_ref, j))
        product = jnp.dot(left, jnp.concatenate([high, low, high], axis=0), preferred_element_type=jnp.float32)
        for start, part in ((j, product[:, :lanes]), (j + half, product[:, lanes:])):
            place = pl.ds(start, rows, segments)
            flat_out[place, :] = flat_panel[place, :] - part
        return carry

    lax.fori_loop(0, half, one, 0, unroll=4)


def update(sums, scale, block_rows, panel_rows):
    def body(*refs):
        update_kernel(scale, *refs)

    return pl.pallas_call(
        body,
        out_shape=jax.ShapeDtypeStruct(panel_rows.shape, jnp.float32),
        compiler_params=pltpu.CompilerParams(vmem_limit_bytes=vmem_bytes),
        cost_estimate=pl.CostEstimate(
            flops=6 * block_rows.shape[0] * panel_rows.size, bytes_accessed=8 * panel_rows.size, transcendentals=0
        ),
        name="update",
    )(sums, block_rows, panel_rows)


def halos(field):
    planes = field.shape[1]
    up = [(i, (i + 1) % 4) for i in range(4)]
    down = [(j, i) for i, j in up]
    before = lax.ppermute(field[:, planes - reach :], ("yh", "c"), up)
    after = lax.ppermute(field[:, :reach], ("yh", "c"), down)
    return before, after


def summed(partial, spots):
    parts = [partial]
    for step in range(1, 4):
        parts.append(lax.ppermute(partial, ("yh", "c"), [(i, i ^ step) for i in range(4)]))
    partial = (parts[0] + parts[1]) + (parts[2] + parts[3])
    copies = jnp.broadcast_to(partial[None], (spots,) + partial.shape)
    return lax.all_to_all(copies, ("z", "x"), 0, 0, tiled=True)


def shards(panels, potential, block_index):
    count, own = panels.shape[:2]
    lanes = panels.shape[-1]
    spots = lax.axis_size("z") * lax.axis_size("x")
    cell_count = lax.axis_size("yh") * lax.axis_size("c") * potential.size

    block = lax.dynamic_index_in_dim(panels, block_index[0], 0, keepdims=False)
    before, after = halos(block)
    sent = jnp.swapaxes(panels.reshape(count * own, spots, -1, lanes), 0, 1)
    panel_rows = lax.all_to_all(sent, ("z", "x"), 0, 0, tiled=True)
    panel_rows = panel_rows.reshape((-1,) + sent.shape[2:])

    (first,) = stencil(before, block, after, potential)
    before, after = halos(first)
    filtered, chunks = stencil(before, first, after, potential, block, (spots, lax.axis_size("yl")))
    chunks, panel_rows = lax.optimization_barrier((chunks, panel_rows))
    chunks = chunks.reshape((-1,) + chunks.shape[2:])
    block_rows = lax.all_to_all(chunks, ("z", "x", "yl"), 0, 0, tiled=True)
    block_rows = block_rows.reshape((-1,) + chunks.shape[2:])

    sums = summed(gram(panel_rows, block_rows), spots)
    fresh = update(sums, 1.0 / cell_count, block_rows, panel_rows)
    home = lax.all_to_all(fresh.reshape(sent.shape), ("z", "x"), 0, 0, tiled=True)
    updated = jnp.swapaxes(home, 0, 1).reshape(panels.shape)
    return filtered, updated


def solution(mesh):
    fine = Mesh(mesh.devices.reshape(4, 4, 2, 2, 2), ("z", "x", "yl", "yh", "c"))
    band, space = ("z", "x", "yl"), ("yh", "c")
    return jax.shard_map(
        shards,
        mesh=fine,
        in_specs=(P(None, band, space, None, None), P(space, None, None), P()),
        out_specs=(P(band, space, None, None), P(None, band, space, None, None)),
        check_vma=False,
    )
```

time: 214 us -> 181 us (0.85)
  waiting for transfers between devices: 78.7 us -> 39.6 us
  blocking collectives: 82.3 us -> 95.2 us
  local copies, waits for them, and re-layouts: 9.92 us -> 6.8 us
  starting transfers between devices: 15.7 us -> 12.6 us
    ppermute x14 -> x7, waiting for transfers between devices: 64.9 us -> 34.9 us  [the longest x2 19.9 us: halos(): after = lax.ppermute(field[:, :reach], ('yh', 'c'), down)]
    all_to_all x2 -> x3, blocking collectives: 82.3 us -> 95.2 us  [the longest x1 42.2 us: shards(): lax.all_to_all(fresh.reshape(sent.shape), ('z', 'x'), 0, 0, tiled=True)]
    all_to_all x1, waiting for transfers between devices: 13.8 us -> 4.64 us  [shards(): panel_rows = lax.all_to_all(sent, ('z', 'x'), 0, 0, tiled=True)]
    reshape x2 -> x1, local copies, waits for them, and re-layouts: 6.29 us -> 1.88 us  [shards(): sent = jnp.swapaxes(panels.reshape(count * own, spots, -1, lanes), 0, 1)]
    ppermute x14 -> x7, starting transfers between devices: 7.06 us -> 4.53 us  [the longest x3 3.44 us: summed(): lax.ppermute(partial, ('yh', 'c'), [(i, i ^ step) for i in range(4)])]
  transfers between devices with their start and end apart: 15 -> 8, of which waited for: 15 -> 7; matrix products, arithmetic and copies ran while one was open for 2% -> 1% of each run, Pallas kernels for 0% -> 6%
where the time goes in v2:
time: 181 us; the launch traced here: 180 us
  blocking collectives  95.2 us (53%)
  waiting for transfers between devices  39.6 us (22%)
  Pallas kernels  24.9 us (14%)
  starting transfers between devices  12.6 us (7%)
  local copies, waits for them, and re-layouts  6.8 us (4%)
    all_to_all x1, blocking collectives, shards(): lax.all_to_all(fresh.reshape(sent.shape), ('z', 'x'), 0, 0, tiled=True)  42.2 us
    all_to_all x1, blocking collectives, shards(): block_rows = lax.all_to_all(chunks, ('z', 'x', 'yl'), 0, 0, tiled=True)  36.7 us
    ppermute x2, waiting for transfers between devices, halos(): after = lax.ppermute(field[:, :reach], ('yh', 'c'), down)  19.9 us
    all_to_all x1, blocking collectives, summed(): return lax.all_to_all(copies, ('z', 'x'), 0, 0, tiled=True)  16.3 us
    ppermute x2, waiting for transfers between devices, halos(): before = lax.ppermute(field[:, planes - reach:], ('yh', 'c'), up)  11.8 us
    pallas_call x2, Pallas kernels, stencil(): pl.pallas_call(body, grid=(bands,), in_specs=specs, out_specs=out_specs,...  10.8 us
    all_to_all x1, starting transfers between devices, shards(): panel_rows = lax.all_to_all(sent, ('z', 'x'), 0, 0, tiled=True)  8.05 us
    pallas_call x1, Pallas kernels, update(): pl.pallas_call(body, out_shape=jax.ShapeDtypeStruct(panel_rows.shape, jnp...  7.31 us
  transfers between devices with their start and end apart: 8, of which 7 were waited for; matrix products, arithmetic and copies ran while one was open for 1% of the time, Pallas kernels for 6%

profile of v2, /device:TPU:16, one launch (start us, length us, event | category | flops | bytes accessed | tf_op | source)
XLA Modules:
  0.0 180.5 jit_solution(2090229318374373565)
XLA Ops:
  1.3 0.0 copy-start.1
  1.3 1.4 dynamic-slice_bitcast_fusion.refs_1_.refs_4_
  2.7 1.4 fusion.1
  4.1 0.0 collective-permute-start.1
  4.1 0.5 collective-permute-start
  4.6 0.0 copy-done.1
  4.6 1.9 %copy.8 = f32[6,16,64,128]{3,2,0,1:T(8,128)} copy(f32[6,16,64,128]{3,2,1,0:T(8,128)S(1)} %bitcast.21) | data formatting | bytes 6291456 | tf_op jit(solution)/shard_map/reshape | solution.py:198
  6.5 0.0 copy-start
  6.5 8.1 %all-to-all-start = ((f32[16,6,64,128]{3,2,1,0:T(8,128)}), f32[16,6,64,128]{3,2,1,0:T(8,128)}, u32[]{:S(2)}, u32[]{:S(2)}) async-start(f32[16,6,64,128]{3,2,1,0:T(8,128)} %bitcast.19), calls=%async_computation | async-start | bytes 6291456 | tf_op jit(solution)/shard_map/all_to_all | solution.py:199
  14.6 5.3 %collective-permute-done.1.refs_2_ = f32[2,6,128,128]{3,2,1,0:T(8,128)S(1)} collective-permute-done((f32[2,6,128,128]{3,2,1,0:T(8,128)}, f32[2,6,128,128]{3,2,1,0:T(8,128)S(1)}, u32[]{:S(2)}, u32[]{:S(2)}) %collective-permute-start.1) | collective-permute-done | bytes 786464 | tf_op jit(solution)/shard_map/ppermute | solution.py:177
  19.9 5.8 %collective-permute-done.refs_0_ = f32[2,6,128,128]{3,2,1,0:T(8,128)S(1)} collective-permute-done((f32[2,6,128,128]{3,2,1,0:T(8,128)}, f32[2,6,128,128]{3,2,1,0:T(8,128)S(1)}, u32[]{:S(2)}, u32[]{:S(2)}) %collective-permute-start) | collective-permute-done | bytes 786464 | tf_op jit(solution)/shard_map/ppermute | solution.py:176
  25.7 0.0 copy-done
  25.7 4.8 %stencil.2.refs_1_ = f32[2,8,128,128]{3,2,1,0:T(8,128)S(1)} custom-call(f32[2,6,128,128]{3,2,1,0:T(8,128)S(1)} %collective-permute-done.refs_0_, f32[2,8,128,128]{3,2,1,0:T(8,128)S(1)} %dynamic-slice_bitcast_fusion.refs_1_.refs_4_, f32[2,6,128,128]{3,2,1,0:T(8,128)S(1)} %collective-permute-done.1.refs_2_, f32[8,128,128]{2,1,0:T(8,128)S(1)} %copy-done), custom_call_target="tpu_custom_call" | custom-call | flops 1310720000000 | bytes 4194304 | tf_op jit(solution)/shard_map/stencil/pallas_call | solution.py:79
  30.4 0.2 fusion
  30.6 0.1 collective-permute-start.3
  30.7 0.5 collective-permute-start.2
  31.2 14.6 %collective-permute-done.3.refs_2_ = f32[2,6,128,128]{3,2,1,0:T(8,128)S(1)} collective-permute-done((f32[2,6,128,128]{3,2,1,0:T(8,128)S(1)}, f32[2,6,128,128]{3,2,1,0:T(8,128)S(1)}, u32[]{:S(2)}, u32[]{:S(2)}) %collective-permute-start.3) | collective-permute-done | bytes 786464 | tf_op jit(solution)/shard_map/ppermute | solution.py:177
  45.8 6.0 %collective-permute-done.2.refs_0_ = f32[2,6,128,128]{3,2,1,0:T(8,128)S(1)} collective-permute-done((f32[2,6,128,128]{3,2,1,0:T(8,128)S(1)}, f32[2,6,128,128]{3,2,1,0:T(8,128)S(1)}, u32[]{:S(2)}, u32[]{:S(2)}) %collective-permute-start.2) | collective-permute-done | bytes 786464 | tf_op jit(solution)/shard_map/ppermute | solution.py:176
  51.8 6.0 %stencil.3 = (f32[2,8,128,128]{3,2,1,0:T(8,128)}, f32[16,2,2,64,128]{4,3,2,1,0:T(8,128)}) custom-call(f32[2,6,128,128]{3,2,1,0:T(8,128)S(1)} %collective-permute-done.2.refs_0_, f32[2,8,128,128]{3,2,1,0:T(8,128)S(1)} %stencil.2.refs_1_, f32[2,6,128,128]{3,2,1,0:T(8,128)S(1)} %collective-permute-done.3.refs_2_, f32[8,128,128]{2,1,0:T(8,128)S(1)} %copy-done, ...), custom_call_target="tpu_custom_call" | custom-call | flops 13107200 | bytes 4194304 | tf_op jit(solution)/shard_map/stencil/pallas_call | solution.py:79
  57.8 4.6 %all-to-all-done = f32[16,6,64,128]{3,2,1,0:T(8,128)} async-done(((f32[16,6,64,128]{3,2,1,0:T(8,128)}), f32[16,6,64,128]{3,2,1,0:T(8,128)}, u32[]{:S(2)}, u32[]{:S(2)}) %all-to-all-start) | async-done | bytes 3145760 | tf_op jit(solution)/shard_map/all_to_all | solution.py:199
  62.4 36.7 %all_to_all.20 = f32[32,2,64,128]{3,2,1,0:T(8,128)S(1)} all-to-all(f32[32,2,64,128]{3,2,1,0:T(8,128)} %bitcast.23), channel_id=1, replica_groups=mesh['z'=4,'x'=4,'yl'=2,'yh'=2,'c'=2] {'z','x','yl'}, dimensions={0} | all-to-all | bytes 4194304 | tf_op jit(solution)/shard_map/all_to_all | solution.py:207
  99.1 6.8 %gram.1 = f32[64,96]{1,0:T(8,128)S(1)} custom-call(f32[96,64,128]{2,1,0:T(8,128)} %bitcast.4.panel_ref.refs_2_, f32[64,64,128]{2,1,0:T(8,128)S(1)} %bitcast.16), custom_call_target="tpu_custom_call" | custom-call | flops 301989888 | bytes 5242880 | tf_op jit(solution)/shard_map/gram/pallas_call | solution.py:124
  106.0 1.3 collective-permute-start.6
  107.3 1.8 %collective-permute-start.5 = (f32[64,96]{1,0:T(8,128)S(1)}, f32[64,96]{1,0:T(8,128)S(1)}, u32[]{:S(2)}, u32[]{:S(2)}) collective-permute-start(f32[64,96]{1,0:T(8,128)S(1)} %gram.1), channel_id=1, source_target_pairs={{0,2},{1,3},{2,0},{3,1},{4,6},{5,7},{6,4},{7,5},{8,10},{9,11},{10,... | collective-permute-start | bytes 73736 | tf_op jit(solution)/shard_map/ppermute | solution.py:184
  109.1 0.3 collective-permute-start.4
  109.4 1.8 %collective-permute-done.6 = f32[64,96]{1,0:T(8,128)S(1)} collective-permute-done((f32[64,96]{1,0:T(8,128)S(1)}, f32[64,96]{1,0:T(8,128)S(1)}, u32[]{:S(2)}, u32[]{:S(2)}) %collective-permute-start.6) | collective-permute-done | bytes 24608 | tf_op jit(solution)/shard_map/ppermute | solution.py:184
  111.2 1.4 collective-permute-done.5
  112.7 0.0 collective-permute-done.4
  112.7 16.3 %all_to_all.21.refs_0_ = f32[16,64,96]{2,1,0:T(8,128)S(1)} all-to-all(f32[16,64,96]{2,1,0:T(8,128)S(1)} %broadcast_in_dim.2), channel_id=1, replica_groups=mesh['z'=4,'x'=4,'yl'=2,'yh'=2,'c'=2] {'z','x'}, dimensions={0} | all-to-all | bytes 786432 | tf_op jit(solution)/shard_map/all_to_all | solution.py:187
  129.0 7.3 %update.1 = f32[96,64,128]{2,1,0:T(8,128)S(1)} custom-call(f32[16,64,96]{2,1,0:T(8,128)S(1)} %all_to_all.21.refs_0_, f32[64,64,128]{2,1,0:T(8,128)S(1)} %bitcast.17, f32[96,64,128]{2,1,0:T(8,128)} %bitcast.4.panel_ref.refs_2_), custom_call_target="tpu_custom_call" | custom-call | flops 301989888 | bytes 6291456 | tf_op jit(solution)/shard_map/update/pallas_call | solution.py:161
  136.4 42.2 %all_to_all.22 = f32[16,6,64,128]{3,2,1,0:T(8,128)S(1)} all-to-all(f32[16,6,64,128]{3,2,1,0:T(8,128)S(1)} %bitcast.18), channel_id=1, replica_groups=mesh['z'=4,'x'=4,'yl'=2,'yh'=2,'c'=2] {'z','x'}, dimensions={0} | all-to-all | bytes 6291456 | tf_op jit(solution)/shard_map/all_to_all | solution.py:212
  178.6 1.9 %copy.6 = f32[6,16,64,128]{3,2,1,0:T(8,128)} copy(f32[6,16,64,128]{3,2,0,1:T(8,128)S(1)} %bitcast.20) | data formatting | bytes 6291456 | tf_op jit(solution)/shard_map/transpose | solution.py:213
  (2 shorter events, 0.1 us)
Async XLA Ops:
  1.3 3.4 %copy-start.1 = (f32[3,2,8,128,128]{4,3,2,1,0:T(8,128)S(1)}, f32[3,2,8,128,128]{4,3,2,1,0:T(8,128)}, u32[]{:S(2)}) copy-start(f32[3,2,8,128,128]{4,3,2,1,0:T(8,128)} %param.3) | copy-start | bytes 9437188
  4.1 15.8 %collective-permute-start.1 = (f32[2,6,128,128]{3,2,1,0:T(8,128)}, f32[2,6,128,128]{3,2,1,0:T(8,128)S(1)}, u32[]{:S(2)}, u32[]{:S(2)}) collective-permute-start(f32[2,6,128,128]{3,2,1,0:T(8,128)} %get-tuple-element.12), channel_id=1, source_target_pairs={{1,0},{2,1},{3,2},{0,3},{5,4},{6,5},{7,6},{4,7},{9,8},{10,9},{11,1... | collective-permute-start | bytes 2359304 | tf_op jit(solution)/shard_map/ppermute | solution.py:177
  4.1 21.5 %collective-permute-start = (f32[2,6,128,128]{3,2,1,0:T(8,128)}, f32[2,6,128,128]{3,2,1,0:T(8,128)S(1)}, u32[]{:S(2)}, u32[]{:S(2)}) collective-permute-start(f32[2,6,128,128]{3,2,1,0:T(8,128)} %get-tuple-element.13), channel_id=1, source_target_pairs={{0,1},{1,2},{2,3},{3,0},{4,5},{5,6},{6,7},{7,4},{8,9},{9,10},{10,1... | collective-permute-start | bytes 2359304 | tf_op jit(solution)/shard_map/ppermute | solution.py:176
  6.5 19.1 %copy-start = (f32[8,128,128]{2,1,0:T(8,128)S(1)}, f32[8,128,128]{2,1,0:T(8,128)}, u32[]{:S(2)}) copy-start(f32[8,128,128]{2,1,0:T(8,128)} %refs_3_.3) | copy-start | bytes 1572868
  6.5 55.9 %all-to-all-start = ((f32[16,6,64,128]{3,2,1,0:T(8,128)}), f32[16,6,64,128]{3,2,1,0:T(8,128)}, u32[]{:S(2)}, u32[]{:S(2)}) async-start(f32[16,6,64,128]{3,2,1,0:T(8,128)} %bitcast.19), calls=%async_computation | async-start | bytes 6291456 | tf_op jit(solution)/shard_map/all_to_all | solution.py:199
  30.6 15.1 %collective-permute-start.3 = (f32[2,6,128,128]{3,2,1,0:T(8,128)S(1)}, f32[2,6,128,128]{3,2,1,0:T(8,128)S(1)}, u32[]{:S(2)}, u32[]{:S(2)}) collective-permute-start(f32[2,6,128,128]{3,2,1,0:T(8,128)S(1)} %get-tuple-element.10), channel_id=1, source_target_pairs={{1,0},{2,1},{3,2},{0,3},{5,4},{6,5},{7,6},{4,7},{9,8},{10,9},{11,1... | collective-permute-start | bytes 2359304 | tf_op jit(solution)/shard_map/ppermute | solution.py:177
  30.7 21.1 %collective-permute-start.2 = (f32[2,6,128,128]{3,2,1,0:T(8,128)S(1)}, f32[2,6,128,128]{3,2,1,0:T(8,128)S(1)}, u32[]{:S(2)}, u32[]{:S(2)}) collective-permute-start(f32[2,6,128,128]{3,2,1,0:T(8,128)S(1)} %get-tuple-element.11), channel_id=1, source_target_pairs={{0,1},{1,2},{2,3},{3,0},{4,5},{5,6},{6,7},{7,4},{8,9},{9,10},{10,1... | collective-permute-start | bytes 2359304 | tf_op jit(solution)/shard_map/ppermute | solution.py:176
  106.0 5.3 %collective-permute-start.6 = (f32[64,96]{1,0:T(8,128)S(1)}, f32[64,96]{1,0:T(8,128)S(1)}, u32[]{:S(2)}, u32[]{:S(2)}) collective-permute-start(f32[64,96]{1,0:T(8,128)S(1)} %gram.1), channel_id=1, source_target_pairs={{0,3},{1,2},{2,1},{3,0},{4,7},{5,6},{6,5},{7,4},{8,11},{9,10},{10,... | collective-permute-start | bytes 73736 | tf_op jit(solution)/shard_map/ppermute | solution.py:184
  107.3 5.4 %collective-permute-start.5 = (f32[64,96]{1,0:T(8,128)S(1)}, f32[64,96]{1,0:T(8,128)S(1)}, u32[]{:S(2)}, u32[]{:S(2)}) collective-permute-start(f32[64,96]{1,0:T(8,128)S(1)} %gram.1), channel_id=1, source_target_pairs={{0,2},{1,3},{2,0},{3,1},{4,6},{5,7},{6,4},{7,5},{8,10},{9,11},{10,... | collective-permute-start | bytes 73736 | tf_op jit(solution)/shard_map/ppermute | solution.py:184
  109.1 3.6 %collective-permute-start.4 = (f32[64,96]{1,0:T(8,128)S(1)}, f32[64,96]{1,0:T(8,128)S(1)}, u32[]{:S(2)}, u32[]{:S(2)}) collective-permute-start(f32[64,96]{1,0:T(8,128)S(1)} %gram.1), channel_id=1, source_target_pairs={{0,1},{1,0},{2,3},{3,2},{4,5},{5,4},{6,7},{7,6},{8,9},{9,8},{10,11... | collective-permute-start | bytes 73736 | tf_op jit(solution)/shard_map/ppermute | solution.py:184

commit v3 on v2

v3 whole, which is shorter than its diff:
```python
import jax
import jax.numpy as jnp
from jax import lax
from jax.experimental import pallas as pl
from jax.experimental.pallas import tpu as pltpu
from jax.sharding import Mesh, PartitionSpec as P

stencil_weights = (
    -5369.0 / 1800.0,
    12.0 / 7.0,
    -15.0 / 56.0,
    10.0 / 189.0,
    -1.0 / 112.0,
    2.0 / 1925.0,
    -1.0 / 16632.0,
)
reach = 6
kinetic_factor = -0.5 / 0.25
centre_value = 32.25
half_width = 10.75
vmem_bytes = 16 * 1024 * 1024


def inner_kernel(second, index_ref, panels_ref, pot_ref, *rest):
    if second:
        mid_ref, out_ref, held, held_pot, result_ref, before_ref, sems = rest
    else:
        out_ref, held, held_pot, result_ref, sems = rest
    bands, planes, rows, columns = held.shape
    block_ref = panels_ref.at[index_ref[0]]
    moves = [(pot_ref, held_pot)]
    for b in range(bands):
        moves.append(((mid_ref if second else block_ref).at[b], held.at[b]))
        if second:
            moves.append((block_ref.at[b], before_ref.at[b]))
    copies = [pltpu.make_async_copy(*move, sems.at[i]) for i, move in enumerate(moves)]
    for copy in copies:
        copy.start()
    copies[0].wait()
    scale = (2.0 if second else 1.0) / half_width
    leaving = []
    each = 2 if second else 1
    for b in range(bands):
        for copy in copies[1 + each * b : 1 + each * (b + 1)]:
            copy.wait()
        for z in range(planes):
            centre = held[b, z]
            laplace = 3.0 * stencil_weights[0] * centre
            for k in range(1, reach + 1):
                total = pltpu.roll(centre, k, 0) + pltpu.roll(centre, rows - k, 0)
                total = total + (pltpu.roll(centre, k, 1) + pltpu.roll(centre, columns - k, 1))
                if z + k < planes:
                    total = total + held[b, z + k]
                if z - k >= 0:
                    total = total + held[b, z - k]
                laplace = laplace + stencil_weights[k] * total
            applied = kinetic_factor * laplace + held_pot[z] * centre
            term = (applied - centre_value * centre) * scale
            if second:
                term = term - before_ref[b, z]
            result_ref[b, z] = term
        leaving.append(pltpu.make_async_copy(result_ref.at[b], out_ref.at[b], sems.at[5 + b]))
        leaving[b].start()
    for copy in leaving:
        copy.wait()


def outer_kernel(second, part_ref, lo_ref, hi_ref, out_ref, *rest):
    if second:
        chunk_ref, held, held_lo, held_hi, sems = rest
    else:
        held, held_lo, held_hi, sems = rest
    bands, planes, rows, columns = held.shape
    arrivals = []
    for b in range(bands):
        moves = [(part_ref.at[b], held.at[b]), (lo_ref.at[b], held_lo.at[b]), (hi_ref.at[b], held_hi.at[b])]
        copies = [pltpu.make_async_copy(*move, sems.at[3 * b + i]) for i, move in enumerate(moves)]
        for copy in copies:
            copy.start()
        arrivals.append(copies)
    scale = kinetic_factor * (2.0 if second else 1.0) / half_width
    strip = 16
    leaving = []
    for b in range(bands):
        for copy in arrivals[b]:
            copy.wait()

        def one(i, carry, b=b):
            place = pl.ds(pl.multiple_of(i * strip, strip), strip)
            low = [held_lo[b, j, place] for j in range(reach)]
            high = [held_hi[b, j, place] for j in range(reach)]
            for z in range(planes):
                total = held[b, z, place]
                for k in range(1, reach + 1):
                    if z + k >= planes:
                        total = total + (scale * stencil_weights[k]) * high[z + k - planes]
                    if z - k < 0:
                        total = total + (scale * stencil_weights[k]) * low[reach + z - k]
                held[b, z, place] = total
            return carry

        lax.fori_loop(0, rows // strip, one, 0)
        moves = [(held.at[b], out_ref.at[b])]
        if second:
            copies, spots, _, height, _ = chunk_ref.shape
            source = held.at[b].reshape(spots, height, columns)
            moves += [(source, chunk_ref.at[j, :, b]) for j in range(copies)]
        for i, move in enumerate(moves):
            copy = pltpu.make_async_copy(*move, sems.at[3 * bands + 3 * b + i])
            copy.start()
            leaving.append(copy)
    for copy in leaving:
        copy.wait()


hbm = pl.BlockSpec(memory_space=pltpu.HBM)
INNER_WEIGHT = 50
OUTER_WEIGHT = 100000


def inner(index, panels, potential, mid=None):
    shape = panels.shape[1:]
    second = mid is not None
    operands = [panels, potential] + ([mid] if second else [])
    held = pltpu.VMEM(shape, jnp.float32)
    scratch = [held, pltpu.VMEM(shape[1:], jnp.float32), held] + ([held] if second else [])

    def body(*refs):
        inner_kernel(second, *refs)

    size = potential.size * shape[0]
    return pl.pallas_call(
        body,
        in_specs=[pl.BlockSpec(memory_space=pltpu.SMEM)] + [hbm] * len(operands),
        out_specs=hbm,
        out_shape=jax.ShapeDtypeStruct(shape, jnp.float32),
        scratch_shapes=scratch + [pltpu.SemaphoreType.DMA((5 + shape[0],))],
        compiler_params=pltpu.CompilerParams(vmem_limit_bytes=vmem_bytes),
        cost_estimate=pl.CostEstimate(
            flops=(50 if second else INNER_WEIGHT) * size, bytes_accessed=12 * size, transcendentals=0
        ),
        name="inner",
    )(index, *operands)


def outer(part, lo, hi, chunks=None):
    bands, planes, rows, columns = part.shape
    second = chunks is not None
    weight = 10 if second else OUTER_WEIGHT
    out_shape = [jax.ShapeDtypeStruct(part.shape, jnp.float32)]
    if second:
        copies, spots = chunks
        out_shape.append(jax.ShapeDtypeStruct((copies, spots, bands, planes * rows // spots, columns), jnp.float32))
    halo = pltpu.VMEM((bands, reach, rows, columns), jnp.float32)

    def body(*refs):
        outer_kernel(second, *refs)

    return pl.pallas_call(
        body,
        in_specs=[hbm] * 3,
        out_specs=[hbm] * len(out_shape),
        out_shape=out_shape,
        scratch_shapes=[pltpu.VMEM(part.shape, jnp.float32), halo, halo, pltpu.SemaphoreType.DMA((6 * bands,))],
        compiler_params=pltpu.CompilerParams(vmem_limit_bytes=vmem_bytes),
        cost_estimate=pl.CostEstimate(flops=weight * part.size, bytes_accessed=16 * part.size, transcendentals=0),
        name="outer",
    )(part, lo, hi)


def prepare_kernel(index_ref, panel_ref, sent_ref, low_ref, high_ref):
    bands, planes, rows, columns = panel_ref.shape[1:]
    spots, _, height, _ = sent_ref.shape
    for b in range(bands):
        for z in range(planes):
            for i in range(spots // planes):
                sent_ref[z * (spots // planes) + i, b] = panel_ref[0, b, z, i * height : (i + 1) * height]

    @pl.when(pl.program_id(0) == index_ref[0])
    def edges():
        low_ref[...] = panel_ref[0, :, 0:reach]
        high_ref[...] = panel_ref[0, :, planes - reach : planes]


def prepare(index, panels, spots):
    count, bands, planes, rows, columns = panels.shape
    height = planes * rows // spots
    edge = (bands, reach, rows, columns)
    whole = pl.BlockSpec(edge, lambda p: (0, 0, 0, 0))
    return pl.pallas_call(
        prepare_kernel,
        grid=(count,),
        in_specs=[
            pl.BlockSpec(memory_space=pltpu.SMEM),
            pl.BlockSpec((1, bands, planes, rows, columns), lambda p: (p, 0, 0, 0, 0)),
        ],
        out_specs=[pl.BlockSpec((spots, bands, height, columns), lambda p: (0, p, 0, 0)), whole, whole],
        out_shape=[
            jax.ShapeDtypeStruct((spots, count * bands, height, columns), jnp.float32),
            jax.ShapeDtypeStruct(edge, jnp.float32),
            jax.ShapeDtypeStruct(edge, jnp.float32),
        ],
        compiler_params=pltpu.CompilerParams(vmem_limit_bytes=vmem_bytes),
        cost_estimate=pl.CostEstimate(flops=0, bytes_accessed=8 * panels.size, transcendentals=0),
        name="prepare",
    )(index, panels)


def settle_kernel(panel_ref, change_ref, out_ref):
    for i in range(change_ref.shape[0]):
        out_ref[:, i] = panel_ref[:, i] - change_ref[i]


def settle(rows, change):
    count, spots = rows.shape[:2]
    step = spots // 4
    mine = pl.BlockSpec((count, step) + rows.shape[2:], lambda i: (0, i, 0, 0))
    return pl.pallas_call(
        settle_kernel,
        grid=(spots // step,),
        in_specs=[mine, pl.BlockSpec((step, count) + rows.shape[2:], lambda i: (i, 0, 0, 0))],
        out_specs=mine,
        out_shape=jax.ShapeDtypeStruct(rows.shape, jnp.float32),
        compiler_params=pltpu.CompilerParams(vmem_limit_bytes=vmem_bytes),
        cost_estimate=pl.CostEstimate(flops=rows.size, bytes_accessed=12 * rows.size, transcendentals=0),
        name="settle",
    )(rows, change)


def split(value):
    high = value.astype(jnp.bfloat16)
    low = (value - high.astype(jnp.float32)).astype(jnp.bfloat16)
    return high, low


def pair(ref, j):
    rows, segments = ref.shape[:2]
    flat = ref.reshape(rows * segments, ref.shape[2])
    first = flat[pl.ds(j, rows, segments), :]
    other = flat[pl.ds(j + segments // 2, rows, segments), :]
    return jnp.concatenate([first, other], axis=1)


def gram_kernel(panel_ref, block_ref, out_ref, total_ref):
    rows, segments = panel_ref.shape[:2]
    bands = block_ref.shape[0]
    contract = (((1,), (1,)), ((), ()))

    def one(j, total):
        panel_high, panel_low = split(pair(panel_ref, j))
        block_high, block_low = split(pair(block_ref, j))
        both = jnp.concatenate([panel_high, panel_low], axis=0)
        wide = lax.dot_general(both, block_high, contract, preferred_element_type=jnp.float32)
        narrow = lax.dot_general(panel_high, block_low, contract, preferred_element_type=jnp.float32)
        return total + (wide[:rows] + (wide[rows:] + narrow))

    @pl.when(pl.program_id(0) == 0)
    def clear():
        total_ref[...] = jnp.zeros_like(total_ref)

    total = lax.fori_loop(0, segments // 2, one, total_ref[...], unroll=4)
    total_ref[...] = total

    @pl.when(pl.program_id(0) == pl.num_programs(0) - 1)
    def store():
        out_ref[...] = jnp.concatenate([total[: rows // 2], total[rows // 2 :]], axis=1)


def gram(panel_rows, block_rows):
    rows, segments, lanes = panel_rows.shape
    bands = block_rows.shape[0]
    steps = 4

    def part(count):
        return pl.BlockSpec((count, segments // steps, lanes), lambda i: (0, i, 0))

    return pl.pallas_call(
        gram_kernel,
        grid=(steps,),
        in_specs=[part(rows), part(bands)],
        out_specs=pl.BlockSpec((rows // 2, 2 * bands), lambda i: (0, 0)),
        out_shape=jax.ShapeDtypeStruct((rows // 2, 2 * bands), jnp.float32),
        scratch_shapes=[pltpu.VMEM((rows, bands), jnp.float32)],
        compiler_params=pltpu.CompilerParams(vmem_limit_bytes=vmem_bytes),
        cost_estimate=pl.CostEstimate(
            flops=6 * bands * panel_rows.size, bytes_accessed=4 * (panel_rows.size + block_rows.size), transcendentals=0
        ),
        name="gram",
    )(panel_rows, block_rows)


def project_kernel(scale, sums_ref, block_ref, out_ref):
    rows, segments, lanes = out_ref.shape
    bands = block_ref.shape[0]
    total = sums_ref[0]
    for i in range(1, sums_ref.shape[0]):
        total = total + sums_ref[i]
    total = total * scale
    corr_high, corr_low = split(jnp.concatenate([total[:, :bands], total[:, bands:]], axis=0))
    left = jnp.concatenate([corr_high, corr_high, corr_low], axis=1)
    flat_out = out_ref.reshape(rows * segments, lanes)
    half = segments // 2

    def one(j, carry):
        high, low = split(pair(block_ref, j))
        product = jnp.dot(left, jnp.concatenate([high, low, high], axis=0), preferred_element_type=jnp.float32)
        flat_out[pl.ds(j, rows, segments), :] = product[:, :lanes]
        flat_out[pl.ds(j + half, rows, segments), :] = product[:, lanes:]
        return carry

    lax.fori_loop(0, half, one, 0, unroll=4)


def project(sums, scale, block_rows):
    rows = 2 * sums.shape[1]
    shape = (rows,) + block_rows.shape[1:]

    def body(*refs):
        project_kernel(scale, *refs)

    return pl.pallas_call(
        body,
        out_shape=jax.ShapeDtypeStruct(shape, jnp.float32),
        compiler_params=pltpu.CompilerParams(vmem_limit_bytes=vmem_bytes),
        cost_estimate=pl.CostEstimate(
            flops=6 * rows * block_rows.size, bytes_accessed=4 * (rows * 8192 + block_rows.size), transcendentals=0
        ),
        name="project",
    )(sums, block_rows)


plane_axes = ("x", "z")


def exchange(low, high):
    up = [(i, (i + 1) % 4) for i in range(4)]
    down = [(j, i) for i, j in up]
    return lax.ppermute(high, ("yh", "c"), up), lax.ppermute(low, ("yh", "c"), down)


def summed(partial, spots):
    parts = [partial]
    for step in range(1, 4):
        parts.append(lax.ppermute(partial, ("yh", "c"), [(i, i ^ step) for i in range(4)]))
    partial = (parts[0] + parts[1]) + (parts[2] + parts[3])
    copies = jnp.broadcast_to(partial[None], (spots,) + partial.shape)
    return lax.all_to_all(copies, plane_axes, 0, 0, tiled=True)


def shards(panels, potential, block_index):
    count, own = panels.shape[:2]
    lanes = panels.shape[-1]
    spots = lax.axis_size(plane_axes)
    cell_count = lax.axis_size("yh") * lax.axis_size("c") * potential.size

    planes = panels.shape[2]
    rows = panels.reshape(count * own, spots, -1, lanes)
    sent, low, high = prepare(block_index, panels, spots)
    before, after = exchange(low, high)
    panel_rows = lax.all_to_all(sent, plane_axes, 0, 0, tiled=True)
    panel_rows = panel_rows.reshape((-1,) + sent.shape[2:])

    (first,) = outer(inner(block_index, panels, potential), before, after)
    before, after = exchange(first[:, :reach], first[:, planes - reach :])
    part = inner(block_index, panels, potential, first)
    filtered, chunks = outer(part, before, after, (lax.axis_size("yl"), spots))
    chunks, panel_rows = lax.optimization_barrier((chunks, panel_rows))
    chunks = chunks.reshape((-1,) + chunks.shape[2:])
    block_rows = lax.all_to_all(
        chunks, ("yl",) + plane_axes, 0, 0, tiled=True
    )
    block_rows = block_rows.reshape((-1,) + chunks.shape[2:])

    sums = summed(gram(panel_rows, block_rows), spots)
    change = project(sums, 1.0 / cell_count, block_rows)
    home = lax.all_to_all(change.reshape(sent.shape), plane_axes, 0, 0, tiled=True)
    updated = settle(rows, home).reshape(panels.shape)
    return filtered, updated


def solution(mesh):
    fine = Mesh(mesh.devices.reshape(4, 4, 2, 2, 2), ("z", "x", "yl", "yh", "c"))
    band, space = ("z", "x", "yl"), ("yh", "c")
    return jax.shard_map(
        shards,
        mesh=fine,
        in_specs=(P(None, band, space, None, None), P(space, None, None), P()),
        out_specs=(P(band, space, None, None), P(None, band, space, None, None)),
        check_vma=False,
    )
```

time: 181 us -> 171 us (0.945)
  waiting for transfers between devices: 39.6 us -> 25.3 us
  starting transfers between devices: 12.6 us -> 18 us
    ppermute x4, waiting for transfers between devices: 31.7 us -> 20.7 us  [the longest x2 10.6 us: exchange(): lax.ppermute(high, ('yh', 'c'), up)]
    unnamed x4 -> x12, local copies, waits for them, and re-layouts: 0.01 us -> 6.07 us
    ppermute x4, starting transfers between devices: 1.08 us -> 4 us  [the longest x2 3.46 us: exchange(): lax.ppermute(low, ('yh', 'c'), down)]
    ppermute x3, starting transfers between devices: 3.44 us -> 5.88 us  [summed(): lax.ppermute(partial, ('yh', 'c'), [(i, i ^ step) for i in range(4)])]
    all_to_all x1, waiting for transfers between devices: 4.64 us -> 2.51 us  [shards(): panel_rows = lax.all_to_all(sent, plane_axes, 0, 0, tiled=True)]
    reshape x1 -> x0, local copies, waits for them, and re-layouts: 1.88 us -> none  [shards(): sent = jnp.swapaxes(panels.reshape(count * own, spots, -1, lanes), 0, 1)]
    transpose x1 -> x0, local copies, waits for them, and re-layouts: 1.88 us -> none  [shards(): updated = jnp.swapaxes(home, 0, 1).reshape(panels.shape)]
    pallas_call x4 -> x8, Pallas kernels: 24.9 us -> 25.1 us  [the longest x2 8.07 us: inner(): pl.pallas_call(body, in_specs=[pl.BlockSpec(memory_space=pltpu.SMEM)] + [...]
  transfers between devices with their start and end apart: 8 -> 8, of which waited for: 7 -> 5; matrix products, arithmetic and copies ran while one was open for 1% -> 0% of each run, Pallas kernels for 6% -> 7%
where the time goes in v3:
time: 171 us; the launch traced here: 170 us
  blocking collectives  94.1 us (55%)
  waiting for transfers between devices  25.3 us (15%)
  Pallas kernels  25.1 us (15%)
  starting transfers between devices  18 us (11%)
  local copies, waits for them, and re-layouts  6.26 us (4%)
    all_to_all x1, blocking collectives, shards(): lax.all_to_all(change.reshape(sent.shape), plane_axes, 0, 0, tiled=True)  42.7 us
    all_to_all x1, blocking collectives, shards(): block_rows = lax.all_to_all(chunks, ('yl',) + plane_axes, 0, 0, tiled=True)  35.5 us
    all_to_all x1, blocking collectives, summed(): return lax.all_to_all(copies, plane_axes, 0, 0, tiled=True)  15.9 us
    ppermute x2, waiting for transfers between devices, exchange(): lax.ppermute(high, ('yh', 'c'), up)  10.6 us
    ppermute x2, waiting for transfers between devices, exchange(): lax.ppermute(low, ('yh', 'c'), down)  10.1 us
    all_to_all x1, starting transfers between devices, shards(): panel_rows = lax.all_to_all(sent, plane_axes, 0, 0, tiled=True)  8.17 us
    pallas_call x2, Pallas kernels, inner(): pl.pallas_call(body, in_specs=[pl.BlockSpec(memory_space=pltpu.SMEM)] + [...  8.07 us
    unnamed x12, local copies, waits for them, and re-layouts  6.07 us
  transfers between devices with their start and end apart: 8, of which 5 were waited for; matrix products, arithmetic and copies ran while one was open for 0% of the time, Pallas kernels for 7%

profile of v3, /device:TPU:16, one launch (start us, length us, event | category | flops | bytes accessed | tf_op | source)
XLA Modules:
  0.0 170.1 jit_solution(15199268225844523608)
XLA Ops:
  1.3 0.0 copy-start
  1.3 1.9 %copy-done = f32[3,2,8,128,128]{4,3,2,1,0:T(8,128)S(1)} copy-done((f32[3,2,8,128,128]{4,3,2,1,0:T(8,128)S(1)}, f32[3,2,8,128,128]{4,3,2,1,0:T(8,128)}, u32[]{:S(2)}) %copy-start) | copy-done | bytes 3145752
  3.2 1.7 %prepare.1 = (f32[16,6,64,128]{3,2,1,0:T(8,128)S(1)}, f32[2,6,128,128]{3,2,1,0:T(8,128)}, f32[2,6,128,128]{3,2,1,0:T(8,128)}) custom-call(s32[1]{0:T(128)S(6)} %copy.5.refs_0_.index_ref, f32[3,2,8,128,128]{4,3,2,1,0:T(8,128)S(1)} %copy-done), custom_call_target="tpu_custom_call" | custom-call | bytes 6291456 | tf_op jit(solution)/shard_map/prepare/pallas_call | solution.py:190
  4.9 0.0 copy-start.2
  4.9 1.7 copy-done.2
  6.5 0.0 collective-permute-start
  6.5 3.3 %collective-permute-start.1 = (f32[2,6,128,128]{3,2,1,0:T(8,128)}, f32[2,6,128,128]{3,2,1,0:T(8,128)}, u32[]{:S(2)}, u32[]{:S(2)}) collective-permute-start(f32[2,6,128,128]{3,2,1,0:T(8,128)} %get-tuple-element.10), channel_id=1, source_target_pairs={{1,0},{2,1},{3,2},{0,3},{5,4},{6,5},{7,6},{4,7},{9,8},{10,9},{11,1... | collective-permute-start | bytes 2359304 | tf_op jit(solution)/shard_map/ppermute | solution.py:338
  9.8 0.0 copy-start.1
  9.8 8.2 %all-to-all-start = ((f32[16,6,64,128]{3,2,1,0:T(8,128)}), f32[16,6,64,128]{3,2,1,0:T(8,128)}, u32[]{:S(2)}, u32[]{:S(2)}) async-start(f32[16,6,64,128]{3,2,1,0:T(8,128)} %copy-done.2), calls=%async_computation | async-start | bytes 6291456 | tf_op jit(solution)/shard_map/all_to_all | solution.py:360
  18.0 0.0 copy-done.1
  18.0 0.0 copy-start.3
  18.0 1.0 copy-done.3
  19.0 4.0 %inner.2.refs_0_ = f32[2,8,128,128]{3,2,1,0:T(8,128)S(1)} custom-call(s32[1]{0:T(128)S(6)} %copy.5.refs_0_.index_ref, f32[3,2,8,128,128]{4,3,2,1,0:T(8,128)S(1)} %copy-done.1, f32[8,128,128]{2,1,0:T(8,128)S(1)} %copy-done.3), custom_call_target="tpu_custom_call" | custom-call | flops 13107200 | bytes 3145728 | tf_op jit(solution)/shard_map/inner/pallas_call | solution.py:132
  23.1 4.7 %collective-permute-done.refs_1_ = f32[2,6,128,128]{3,2,1,0:T(8,128)} collective-permute-done((f32[2,6,128,128]{3,2,1,0:T(8,128)}, f32[2,6,128,128]{3,2,1,0:T(8,128)}, u32[]{:S(2)}, u32[]{:S(2)}) %collective-permute-start) | collective-permute-done | bytes 786464 | tf_op jit(solution)/shard_map/ppermute | solution.py:338
  27.7 0.0 collective-permute-done.1.refs_2_
  27.7 1.8 %outer.2.refs_3_ = f32[2,8,128,128]{3,2,1,0:T(8,128)S(1)} custom-call(f32[2,8,128,128]{3,2,1,0:T(8,128)S(1)} %inner.2.refs_0_, f32[2,6,128,128]{3,2,1,0:T(8,128)} %collective-permute-done.refs_1_, f32[2,6,128,128]{3,2,1,0:T(8,128)} %collective-permute-done.1.refs_2_), custom_call_target="tpu_custom_call" | custom-call | flops 26214400000 | bytes 4194304 | tf_op jit(solution)/shard_map/outer/pallas_call | solution.py:159
  29.6 0.0 copy-start.4
  29.6 0.2 fusion
  29.8 0.2 collective-permute-start.3
  30.0 0.5 collective-permute-start.2
  30.5 0.1 copy-done.4
  30.6 4.1 %inner.3.refs_0_ = f32[2,8,128,128]{3,2,1,0:T(8,128)S(1)} custom-call(s32[1]{0:T(128)S(6)} %copy.5.refs_0_.index_ref, f32[3,2,8,128,128]{4,3,2,1,0:T(8,128)S(1)} %copy-done.1, f32[8,128,128]{2,1,0:T(8,128)S(1)} %copy-done.4, f32[2,8,128,128]{3,2,1,0:T(8,128)S(1)} %outer.2.refs_3_), custom_call_target="tpu_custom_call" | custom-call | flops 13107200 | bytes 3145728 | tf_op jit(solution)/shard_map/inner/pallas_call | solution.py:132
  34.7 10.1 %collective-permute-done.3.refs_2_ = f32[2,6,128,128]{3,2,1,0:T(8,128)S(1)} collective-permute-done((f32[2,6,128,128]{3,2,1,0:T(8,128)S(1)}, f32[2,6,128,128]{3,2,1,0:T(8,128)S(1)}, u32[]{:S(2)}, u32[]{:S(2)}) %collective-permute-start.3) | collective-permute-done | bytes 786464 | tf_op jit(solution)/shard_map/ppermute | solution.py:338
  44.8 5.9 %collective-permute-done.2.refs_1_ = f32[2,6,128,128]{3,2,1,0:T(8,128)S(1)} collective-permute-done((f32[2,6,128,128]{3,2,1,0:T(8,128)S(1)}, f32[2,6,128,128]{3,2,1,0:T(8,128)S(1)}, u32[]{:S(2)}, u32[]{:S(2)}) %collective-permute-start.2) | collective-permute-done | bytes 786464 | tf_op jit(solution)/shard_map/ppermute | solution.py:338
  50.7 2.3 %outer.3 = (f32[2,8,128,128]{3,2,1,0:T(8,128)}, f32[2,16,2,64,128]{4,3,2,1,0:T(8,128)S(1)}) custom-call(f32[2,8,128,128]{3,2,1,0:T(8,128)S(1)} %inner.3.refs_0_, f32[2,6,128,128]{3,2,1,0:T(8,128)S(1)} %collective-permute-done.2.refs_1_, f32[2,6,128,128]{3,2,1,0:T(8,128)S(1)} %collective-permute-done.3.refs_2_), custom_call_target="tpu_custom_call" | custom-call | flops 2621440 | bytes 4194304 | tf_op jit(solution)/shard_map/outer/pallas_call | solution.py:159
  53.0 0.0 copy-start.5
  53.1 1.3 copy-done.5
  54.4 2.5 %all-to-all-done = f32[16,6,64,128]{3,2,1,0:T(8,128)} async-done(((f32[16,6,64,128]{3,2,1,0:T(8,128)}), f32[16,6,64,128]{3,2,1,0:T(8,128)}, u32[]{:S(2)}, u32[]{:S(2)}) %all-to-all-start) | async-done | bytes 3145760 | tf_op jit(solution)/shard_map/all_to_all | solution.py:360
  56.9 35.5 %all_to_all.20 = f32[32,2,64,128]{3,2,1,0:T(8,128)S(1)} all-to-all(f32[32,2,64,128]{3,2,1,0:T(8,128)} %bitcast.10), channel_id=1, replica_groups=mesh['z'=4,'x'=4,'yl'=2,'yh'=2,'c'=2] {'yl','x','z'}, dimensions={0} | all-to-all | bytes 4194304 | tf_op jit(solution)/shard_map/all_to_all | solution.py:369
  92.4 4.7 %gram.1 = f32[48,128]{1,0:T(8,128)S(1)} custom-call(f32[96,64,128]{2,1,0:T(8,128)} %bitcast.1.panel_ref, f32[64,64,128]{2,1,0:T(8,128)S(1)} %bitcast.7), custom_call_target="tpu_custom_call" | custom-call | flops 301989888 | bytes 5242880 | tf_op jit(solution)/shard_map/gram/pallas_call | solution.py:277
  97.0 2.6 %collective-permute-start.6 = (f32[48,128]{1,0:T(8,128)S(1)}, f32[48,128]{1,0:T(8,128)S(1)}, u32[]{:S(2)}, u32[]{:S(2)}) collective-permute-start(f32[48,128]{1,0:T(8,128)S(1)} %gram.1), channel_id=1, source_target_pairs={{0,3},{1,2},{2,1},{3,0},{4,7},{5,6},{6,5},{7,4},{8,11},{9,10},{10,... | collective-permute-start | bytes 73736 | tf_op jit(solution)/shard_map/ppermute | solution.py:344
  99.6 3.3 %collective-permute-start.5 = (f32[48,128]{1,0:T(8,128)S(1)}, f32[48,128]{1,0:T(8,128)S(1)}, u32[]{:S(2)}, u32[]{:S(2)}) collective-permute-start(f32[48,128]{1,0:T(8,128)S(1)} %gram.1), channel_id=1, source_target_pairs={{0,2},{1,3},{2,0},{3,1},{4,6},{5,7},{6,4},{7,5},{8,10},{9,11},{10,... | collective-permute-start | bytes 73736 | tf_op jit(solution)/shard_map/ppermute | solution.py:344
  102.9 0.0 collective-permute-start.4
  102.9 0.0 collective-permute-done.6
  102.9 2.0 %collective-permute-done.5 = f32[48,128]{1,0:T(8,128)S(1)} collective-permute-done((f32[48,128]{1,0:T(8,128)S(1)}, f32[48,128]{1,0:T(8,128)S(1)}, u32[]{:S(2)}, u32[]{:S(2)}) %collective-permute-start.5) | collective-permute-done | bytes 24608 | tf_op jit(solution)/shard_map/ppermute | solution.py:344
  104.9 0.0 collective-permute-done.4
  105.0 15.9 %all_to_all.21.refs_0_ = f32[16,48,128]{2,1,0:T(8,128)S(1)} all-to-all(f32[16,48,128]{2,1,0:T(8,128)S(1)} %broadcast_in_dim.2), channel_id=1, replica_groups=mesh['z'=4,'x'=4,'yl'=2,'yh'=2,'c'=2] {'x','z'}, dimensions={0} | all-to-all | bytes 786432 | tf_op jit(solution)/shard_map/all_to_all | solution.py:347
  120.9 4.1 %project.1 = f32[96,64,128]{2,1,0:T(8,128)S(1)} custom-call(f32[16,48,128]{2,1,0:T(8,128)S(1)} %all_to_all.21.refs_0_, f32[64,64,128]{2,1,0:T(8,128)S(1)} %bitcast.8), custom_call_target="tpu_custom_call" | custom-call | flops 301989888 | bytes 5242880 | tf_op jit(solution)/shard_map/project/pallas_call | solution.py:321
  125.0 42.7 %all_to_all.22.change_ref = f32[16,6,64,128]{3,2,1,0:T(8,128)S(1)} all-to-all(f32[16,6,64,128]{3,2,1,0:T(8,128)S(1)} %bitcast.9), channel_id=1, replica_groups=mesh['z'=4,'x'=4,'yl'=2,'yh'=2,'c'=2] {'x','z'}, dimensions={0} | all-to-all | bytes 6291456 | tf_op jit(solution)/shard_map/all_to_all | solution.py:376
  167.8 2.4 %settle.1 = f32[6,16,64,128]{3,2,1,0:T(8,128)} custom-call(f32[6,16,64,128]{3,2,1,0:T(8,128)S(1)} %bitcast.6, f32[16,6,64,128]{3,2,1,0:T(8,128)S(1)} %all_to_all.22.change_ref), custom_call_target="tpu_custom_call" | custom-call | flops 786432 | bytes 9437184 | tf_op jit(solution)/shard_map/settle/pallas_call | solution.py:218
  (2 shorter events, 0.0 us)
Async XLA Ops:
  1.3 1.9 %copy-start = (f32[3,2,8,128,128]{4,3,2,1,0:T(8,128)S(1)}, f32[3,2,8,128,128]{4,3,2,1,0:T(8,128)}, u32[]{:S(2)}) copy-start(f32[3,2,8,128,128]{4,3,2,1,0:T(8,128)} %refs_1_.3) | copy-start | bytes 9437188
  4.9 1.7 copy-start.2
  6.5 21.2 %collective-permute-start = (f32[2,6,128,128]{3,2,1,0:T(8,128)}, f32[2,6,128,128]{3,2,1,0:T(8,128)}, u32[]{:S(2)}, u32[]{:S(2)}) collective-permute-start(f32[2,6,128,128]{3,2,1,0:T(8,128)} %get-tuple-element.9), channel_id=1, source_target_pairs={{0,1},{1,2},{2,3},{3,0},{4,5},{5,6},{6,7},{7,4},{8,9},{9,10},{10,1... | collective-permute-start | bytes 2359304 | tf_op jit(solution)/shard_map/ppermute | solution.py:338
  6.5 21.2 %collective-permute-start.1 = (f32[2,6,128,128]{3,2,1,0:T(8,128)}, f32[2,6,128,128]{3,2,1,0:T(8,128)}, u32[]{:S(2)}, u32[]{:S(2)}) collective-permute-start(f32[2,6,128,128]{3,2,1,0:T(8,128)} %get-tuple-element.10), channel_id=1, source_target_pairs={{1,0},{2,1},{3,2},{0,3},{5,4},{6,5},{7,6},{4,7},{9,8},{10,9},{11,1... | collective-permute-start | bytes 2359304 | tf_op jit(solution)/shard_map/ppermute | solution.py:338
  9.8 8.2 %copy-start.1 = (f32[3,2,8,128,128]{4,3,2,1,0:T(8,128)S(1)}, f32[3,2,8,128,128]{4,3,2,1,0:T(8,128)}, u32[]{:S(2)}) copy-start(f32[3,2,8,128,128]{4,3,2,1,0:T(8,128)} %refs_1_.3) | copy-start | bytes 9437188
  9.8 47.1 %all-to-all-start = ((f32[16,6,64,128]{3,2,1,0:T(8,128)}), f32[16,6,64,128]{3,2,1,0:T(8,128)}, u32[]{:S(2)}, u32[]{:S(2)}) async-start(f32[16,6,64,128]{3,2,1,0:T(8,128)} %copy-done.2), calls=%async_computation | async-start | bytes 6291456 | tf_op jit(solution)/shard_map/all_to_all | solution.py:360
  18.0 1.0 copy-start.3
  29.6 1.0 copy-start.4
  29.8 15.1 %collective-permute-start.3 = (f32[2,6,128,128]{3,2,1,0:T(8,128)S(1)}, f32[2,6,128,128]{3,2,1,0:T(8,128)S(1)}, u32[]{:S(2)}, u32[]{:S(2)}) collective-permute-start(f32[2,6,128,128]{3,2,1,0:T(8,128)S(1)} %get-tuple-element.16), channel_id=1, source_target_pairs={{1,0},{2,1},{3,2},{0,3},{5,4},{6,5},{7,6},{4,7},{9,8},{10,9},{11,1... | collective-permute-start | bytes 2359304 | tf_op jit(solution)/shard_map/ppermute | solution.py:338
  30.0 20.8 %collective-permute-start.2 = (f32[2,6,128,128]{3,2,1,0:T(8,128)S(1)}, f32[2,6,128,128]{3,2,1,0:T(8,128)S(1)}, u32[]{:S(2)}, u32[]{:S(2)}) collective-permute-start(f32[2,6,128,128]{3,2,1,0:T(8,128)S(1)} %get-tuple-element.17), channel_id=1, source_target_pairs={{0,1},{1,2},{2,3},{3,0},{4,5},{5,6},{6,7},{7,4},{8,9},{9,10},{10,1... | collective-permute-start | bytes 2359304 | tf_op jit(solution)/shard_map/ppermute | solution.py:338
  53.0 1.4 copy-start.5
  97.0 5.9 %collective-permute-start.6 = (f32[48,128]{1,0:T(8,128)S(1)}, f32[48,128]{1,0:T(8,128)S(1)}, u32[]{:S(2)}, u32[]{:S(2)}) collective-permute-start(f32[48,128]{1,0:T(8,128)S(1)} %gram.1), channel_id=1, source_target_pairs={{0,3},{1,2},{2,1},{3,0},{4,7},{5,6},{6,5},{7,4},{8,11},{9,10},{10,... | collective-permute-start | bytes 73736 | tf_op jit(solution)/shard_map/ppermute | solution.py:344
  99.6 5.3 %collective-permute-start.5 = (f32[48,128]{1,0:T(8,128)S(1)}, f32[48,128]{1,0:T(8,128)S(1)}, u32[]{:S(2)}, u32[]{:S(2)}) collective-permute-start(f32[48,128]{1,0:T(8,128)S(1)} %gram.1), channel_id=1, source_target_pairs={{0,2},{1,3},{2,0},{3,1},{4,6},{5,7},{6,4},{7,5},{8,10},{9,11},{10,... | collective-permute-start | bytes 73736 | tf_op jit(solution)/shard_map/ppermute | solution.py:344
  102.9 2.1 %collective-permute-start.4 = (f32[48,128]{1,0:T(8,128)S(1)}, f32[48,128]{1,0:T(8,128)S(1)}, u32[]{:S(2)}, u32[]{:S(2)}) collective-permute-start(f32[48,128]{1,0:T(8,128)S(1)} %gram.1), channel_id=1, source_target_pairs={{0,1},{1,0},{2,3},{3,2},{4,5},{5,4},{6,7},{7,6},{8,9},{9,8},{10,11... | collective-permute-start | bytes 73736 | tf_op jit(solution)/shard_map/ppermute | solution.py:344

commit v4 on v3

--- a/solution.py
+++ b/solution.py
@@ -168,39 +168,41 @@
     )(part, lo, hi)
 
 
-def prepare_kernel(index_ref, panel_ref, sent_ref, low_ref, high_ref):
-    bands, planes, rows, columns = panel_ref.shape[1:]
+def prepare_kernel(index_ref, panels_ref, sent_ref, low_ref, high_ref, held, sems):
+    count, bands, planes, rows, columns = held.shape
     spots, _, height, _ = sent_ref.shape
-    for b in range(bands):
-        for z in range(planes):
-            for i in range(spots // planes):
-                sent_ref[z * (spots // planes) + i, b] = panel_ref[0, b, z, i * height : (i + 1) * height]
-
-    @pl.when(pl.program_id(0) == index_ref[0])
-    def edges():
-        low_ref[...] = panel_ref[0, :, 0:reach]
-        high_ref[...] = panel_ref[0, :, planes - reach : planes]
+    arrivals = [pltpu.make_async_copy(panels_ref.at[p], held.at[p], sems.at[p]) for p in range(count)]
+    for copy in arrivals:
+        copy.start()
+    leaving = []
+
+    def leave(source, target):
+        copy = pltpu.make_async_copy(source, target, sems.at[count + len(leaving)])
+        copy.start()
+        leaving.append(copy)
+
+    for p in range(count):
+        arrivals[p].wait()
+        for b in range(bands):
+            leave(held.at[p, b].reshape(spots, height, columns), sent_ref.at[:, p * bands + b])
+    block = held.at[index_ref[0]]
+    leave(block.at[:, 0:reach], low_ref)
+    leave(block.at[:, planes - reach : planes], high_ref)
+    for copy in leaving:
+        copy.wait()
 
 
 def prepare(index, panels, spots):
     count, bands, planes, rows, columns = panels.shape
     height = planes * rows // spots
-    edge = (bands, reach, rows, columns)
-    whole = pl.BlockSpec(edge, lambda p: (0, 0, 0, 0))
+    edge = jax.ShapeDtypeStruct((bands, reach, rows, columns), jnp.float32)
     return pl.pallas_call(
         prepare_kernel,
-        grid=(count,),
-        in_specs=[
-            pl.BlockSpec(memory_space=pltpu.SMEM),
-            pl.BlockSpec((1, bands, planes, rows, columns), lambda p: (p, 0, 0, 0, 0)),
-        ],
-        out_specs=[pl.BlockSpec((spots, bands, height, columns), lambda p: (0, p, 0, 0)), whole, whole],
-        out_shape=[
-            jax.ShapeDtypeStruct((spots, count * bands, height, columns), jnp.float32),
-            jax.ShapeDtypeStruct(edge, jnp.float32),
-            jax.ShapeDtypeStruct(edge, jnp.float32),
-        ],
-        compiler_params=pltpu.CompilerParams(vmem_limit_bytes=vmem_bytes),
+        in_specs=[pl.BlockSpec(memory_space=pltpu.SMEM), hbm],
+        out_specs=[hbm] * 3,
+        out_shape=[jax.ShapeDtypeStruct((spots, count * bands, height, columns), jnp.float32), edge, edge],
+        scratch_shapes=[pltpu.VMEM(panels.shape, jnp.float32), pltpu.SemaphoreType.DMA((count + count * bands + 2,))],
+        compiler_params=pltpu.CompilerParams(vmem_limit_bytes=62 * 1024 * 1024),
         cost_estimate=pl.CostEstimate(flops=0, bytes_accessed=8 * panels.size, transcendentals=0),
         name="prepare",
     )(index, panels)
@@ -213,7 +215,7 @@
 
 def settle(rows, change):
     count, spots = rows.shape[:2]
-    step = spots // 4
+    step = spots // 2
     mine = pl.BlockSpec((count, step) + rows.shape[2:], lambda i: (0, i, 0, 0))
     return pl.pallas_call(
         settle_kernel,

time: 171 us -> 169 us (0.988)
  local copies, waits for them, and re-layouts: 6.26 us -> 2.72 us
    unnamed x12 -> x8, local copies, waits for them, and re-layouts: 6.07 us -> 2.53 us
    pallas_call x1, Pallas kernels: 1.71 us -> 3.52 us  [prepare(): pl.pallas_call(prepare_kernel, in_specs=[pl.BlockSpec(memory_space=pltpu....]
where the time goes in v4:
time: 169 us; the launch traced here: 168 us
  blocking collectives  94 us (56%)
  Pallas kernels  26.6 us (16%)
  waiting for transfers between devices  25.4 us (15%)
  starting transfers between devices  18.1 us (11%)
  local copies, waits for them, and re-layouts  2.72 us (2%)
    all_to_all x1, blocking collectives, shards(): lax.all_to_all(change.reshape(sent.shape), plane_axes, 0, 0, tiled=True)  42.7 us
    all_to_all x1, blocking collectives, shards(): block_rows = lax.all_to_all(chunks, ('yl',) + plane_axes, 0, 0, tiled=True)  35.4 us
    all_to_all x1, blocking collectives, summed(): return lax.all_to_all(copies, plane_axes, 0, 0, tiled=True)  15.9 us
    ppermute x2, waiting for transfers between devices, exchange(): lax.ppermute(high, ('yh', 'c'), up)  10.6 us
    ppermute x2, waiting for transfers between devices, exchange(): lax.ppermute(low, ('yh', 'c'), down)  10.1 us
    all_to_all x1, starting transfers between devices, shards(): panel_rows = lax.all_to_all(sent, plane_axes, 0, 0, tiled=True)  8.17 us
    pallas_call x2, Pallas kernels, inner(): pl.pallas_call(body, in_specs=[pl.BlockSpec(memory_space=pltpu.SMEM)] + [...  8.07 us
    ppermute x3, starting transfers between devices, summed(): lax.ppermute(partial, ('yh', 'c'), [(i, i ^ step) for i in range(4)])  5.87 us
  transfers between devices with their start and end apart: 8, of which 5 were waited for; matrix products, arithmetic and copies ran while one was open for 0% of the time, Pallas kernels for 7%

profile of v4, /device:TPU:16, one launch (start us, length us, event | category | flops | bytes accessed | tf_op | source)
XLA Modules:
  0.0 168.1 jit_solution(13978641718597310913)
XLA Ops:
  1.3 3.5 %prepare.1 = (f32[16,6,64,128]{3,2,1,0:T(8,128)}, f32[2,6,128,128]{3,2,1,0:T(8,128)}, f32[2,6,128,128]{3,2,1,0:T(8,128)}) custom-call(s32[1]{0:T(128)S(6)} %copy.5.refs_0_.index_ref, f32[3,2,8,128,128]{4,3,2,1,0:T(8,128)} %refs_1_.3), custom_call_target="tpu_custom_call" | custom-call | bytes 6291456 | tf_op jit(solution)/shard_map/prepare/pallas_call | solution.py:199
  4.8 0.1 collective-permute-start
  4.9 3.2 %collective-permute-start.1 = (f32[2,6,128,128]{3,2,1,0:T(8,128)}, f32[2,6,128,128]{3,2,1,0:T(8,128)}, u32[]{:S(2)}, u32[]{:S(2)}) collective-permute-start(f32[2,6,128,128]{3,2,1,0:T(8,128)} %get-tuple-element.10), channel_id=1, source_target_pairs={{1,0},{2,1},{3,2},{0,3},{5,4},{6,5},{7,6},{4,7},{9,8},{10,9},{11,1... | collective-permute-start | bytes 2359304 | tf_op jit(solution)/shard_map/ppermute | solution.py:340
  8.1 0.0 copy-start
  8.1 8.2 %all-to-all-start = ((f32[16,6,64,128]{3,2,1,0:T(8,128)}), f32[16,6,64,128]{3,2,1,0:T(8,128)}, u32[]{:S(2)}, u32[]{:S(2)}) async-start(f32[16,6,64,128]{3,2,1,0:T(8,128)} %get-tuple-element.13), calls=%async_computation | async-start | bytes 6291456 | tf_op jit(solution)/shard_map/all_to_all | solution.py:362
  16.3 0.0 copy-done
  16.3 0.0 copy-start.1
  16.3 1.0 copy-done.1
  17.4 4.0 %inner.2.refs_0_ = f32[2,8,128,128]{3,2,1,0:T(8,128)S(1)} custom-call(s32[1]{0:T(128)S(6)} %copy.5.refs_0_.index_ref, f32[3,2,8,128,128]{4,3,2,1,0:T(8,128)S(1)} %copy-done, f32[8,128,128]{2,1,0:T(8,128)S(1)} %copy-done.1), custom_call_target="tpu_custom_call" | custom-call | flops 13107200 | bytes 3145728 | tf_op jit(solution)/shard_map/inner/pallas_call | solution.py:132
  21.4 4.7 %collective-permute-done.refs_1_ = f32[2,6,128,128]{3,2,1,0:T(8,128)} collective-permute-done((f32[2,6,128,128]{3,2,1,0:T(8,128)}, f32[2,6,128,128]{3,2,1,0:T(8,128)}, u32[]{:S(2)}, u32[]{:S(2)}) %collective-permute-start) | collective-permute-done | bytes 786464 | tf_op jit(solution)/shard_map/ppermute | solution.py:340
  26.1 0.0 collective-permute-done.1.refs_2_
  26.1 1.8 %outer.2.refs_3_ = f32[2,8,128,128]{3,2,1,0:T(8,128)S(1)} custom-call(f32[2,8,128,128]{3,2,1,0:T(8,128)S(1)} %inner.2.refs_0_, f32[2,6,128,128]{3,2,1,0:T(8,128)} %collective-permute-done.refs_1_, f32[2,6,128,128]{3,2,1,0:T(8,128)} %collective-permute-done.1.refs_2_), custom_call_target="tpu_custom_call" | custom-call | flops 26214400000 | bytes 4194304 | tf_op jit(solution)/shard_map/outer/pallas_call | solution.py:159
  27.9 0.0 copy-start.2
  27.9 0.2 fusion
  28.1 0.2 collective-permute-start.3
  28.3 0.5 collective-permute-start.2
  28.8 0.1 copy-done.2
  29.0 4.1 %inner.3.refs_0_ = f32[2,8,128,128]{3,2,1,0:T(8,128)S(1)} custom-call(s32[1]{0:T(128)S(6)} %copy.5.refs_0_.index_ref, f32[3,2,8,128,128]{4,3,2,1,0:T(8,128)S(1)} %copy-done, f32[8,128,128]{2,1,0:T(8,128)S(1)} %copy-done.2, f32[2,8,128,128]{3,2,1,0:T(8,128)S(1)} %outer.2.refs_3_), custom_call_target="tpu_custom_call" | custom-call | flops 13107200 | bytes 3145728 | tf_op jit(solution)/shard_map/inner/pallas_call | solution.py:132
  33.0 10.1 %collective-permute-done.3.refs_2_ = f32[2,6,128,128]{3,2,1,0:T(8,128)S(1)} collective-permute-done((f32[2,6,128,128]{3,2,1,0:T(8,128)S(1)}, f32[2,6,128,128]{3,2,1,0:T(8,128)S(1)}, u32[]{:S(2)}, u32[]{:S(2)}) %collective-permute-start.3) | collective-permute-done | bytes 786464 | tf_op jit(solution)/shard_map/ppermute | solution.py:340
  43.2 5.9 %collective-permute-done.2.refs_1_ = f32[2,6,128,128]{3,2,1,0:T(8,128)S(1)} collective-permute-done((f32[2,6,128,128]{3,2,1,0:T(8,128)S(1)}, f32[2,6,128,128]{3,2,1,0:T(8,128)S(1)}, u32[]{:S(2)}, u32[]{:S(2)}) %collective-permute-start.2) | collective-permute-done | bytes 786464 | tf_op jit(solution)/shard_map/ppermute | solution.py:340
  49.1 2.3 %outer.3 = (f32[2,8,128,128]{3,2,1,0:T(8,128)}, f32[2,16,2,64,128]{4,3,2,1,0:T(8,128)S(1)}) custom-call(f32[2,8,128,128]{3,2,1,0:T(8,128)S(1)} %inner.3.refs_0_, f32[2,6,128,128]{3,2,1,0:T(8,128)S(1)} %collective-permute-done.2.refs_1_, f32[2,6,128,128]{3,2,1,0:T(8,128)S(1)} %collective-permute-done.3.refs_2_), custom_call_target="tpu_custom_call" | custom-call | flops 2621440 | bytes 4194304 | tf_op jit(solution)/shard_map/outer/pallas_call | solution.py:159
  51.4 0.0 copy-start.3
  51.4 1.4 copy-done.3
  52.7 2.6 %all-to-all-done = f32[16,6,64,128]{3,2,1,0:T(8,128)} async-done(((f32[16,6,64,128]{3,2,1,0:T(8,128)}), f32[16,6,64,128]{3,2,1,0:T(8,128)}, u32[]{:S(2)}, u32[]{:S(2)}) %all-to-all-start) | async-done | bytes 3145760 | tf_op jit(solution)/shard_map/all_to_all | solution.py:362
  55.3 35.4 %all_to_all.20 = f32[32,2,64,128]{3,2,1,0:T(8,128)S(1)} all-to-all(f32[32,2,64,128]{3,2,1,0:T(8,128)} %bitcast.10), channel_id=1, replica_groups=mesh['z'=4,'x'=4,'yl'=2,'yh'=2,'c'=2] {'yl','x','z'}, dimensions={0} | all-to-all | bytes 4194304 | tf_op jit(solution)/shard_map/all_to_all | solution.py:371
  90.7 4.7 %gram.1 = f32[48,128]{1,0:T(8,128)S(1)} custom-call(f32[96,64,128]{2,1,0:T(8,128)} %bitcast.1.panel_ref, f32[64,64,128]{2,1,0:T(8,128)S(1)} %bitcast.7), custom_call_target="tpu_custom_call" | custom-call | flops 301989888 | bytes 5242880 | tf_op jit(solution)/shard_map/gram/pallas_call | solution.py:279
  95.4 2.6 %collective-permute-start.6 = (f32[48,128]{1,0:T(8,128)S(1)}, f32[48,128]{1,0:T(8,128)S(1)}, u32[]{:S(2)}, u32[]{:S(2)}) collective-permute-start(f32[48,128]{1,0:T(8,128)S(1)} %gram.1), channel_id=1, source_target_pairs={{0,3},{1,2},{2,1},{3,0},{4,7},{5,6},{6,5},{7,4},{8,11},{9,10},{10,... | collective-permute-start | bytes 73736 | tf_op jit(solution)/shard_map/ppermute | solution.py:346
  97.9 3.3 %collective-permute-start.5 = (f32[48,128]{1,0:T(8,128)S(1)}, f32[48,128]{1,0:T(8,128)S(1)}, u32[]{:S(2)}, u32[]{:S(2)}) collective-permute-start(f32[48,128]{1,0:T(8,128)S(1)} %gram.1), channel_id=1, source_target_pairs={{0,2},{1,3},{2,0},{3,1},{4,6},{5,7},{6,4},{7,5},{8,10},{9,11},{10,... | collective-permute-start | bytes 73736 | tf_op jit(solution)/shard_map/ppermute | solution.py:346
  101.2 0.0 collective-permute-start.4
  101.2 0.0 collective-permute-done.6
  101.2 2.0 %collective-permute-done.5 = f32[48,128]{1,0:T(8,128)S(1)} collective-permute-done((f32[48,128]{1,0:T(8,128)S(1)}, f32[48,128]{1,0:T(8,128)S(1)}, u32[]{:S(2)}, u32[]{:S(2)}) %collective-permute-start.5) | collective-permute-done | bytes 24608 | tf_op jit(solution)/shard_map/ppermute | solution.py:346
  103.3 0.0 collective-permute-done.4
  103.3 15.9 %all_to_all.21.refs_0_ = f32[16,48,128]{2,1,0:T(8,128)S(1)} all-to-all(f32[16,48,128]{2,1,0:T(8,128)S(1)} %broadcast_in_dim.2), channel_id=1, replica_groups=mesh['z'=4,'x'=4,'yl'=2,'yh'=2,'c'=2] {'x','z'}, dimensions={0} | all-to-all | bytes 786432 | tf_op jit(solution)/shard_map/all_to_all | solution.py:349
  119.2 4.1 %project.1 = f32[96,64,128]{2,1,0:T(8,128)S(1)} custom-call(f32[16,48,128]{2,1,0:T(8,128)S(1)} %all_to_all.21.refs_0_, f32[64,64,128]{2,1,0:T(8,128)S(1)} %bitcast.8), custom_call_target="tpu_custom_call" | custom-call | flops 301989888 | bytes 5242880 | tf_op jit(solution)/shard_map/project/pallas_call | solution.py:323
  123.3 42.7 %all_to_all.22.change_ref = f32[16,6,64,128]{3,2,1,0:T(8,128)S(1)} all-to-all(f32[16,6,64,128]{3,2,1,0:T(8,128)S(1)} %bitcast.9), channel_id=1, replica_groups=mesh['z'=4,'x'=4,'yl'=2,'yh'=2,'c'=2] {'x','z'}, dimensions={0} | all-to-all | bytes 6291456 | tf_op jit(solution)/shard_map/all_to_all | solution.py:378
  166.1 2.0 %settle.1 = f32[6,16,64,128]{3,2,1,0:T(8,128)} custom-call(f32[6,16,64,128]{3,2,1,0:T(8,128)S(1)} %bitcast.6, f32[16,6,64,128]{3,2,1,0:T(8,128)S(1)} %all_to_all.22.change_ref), custom_call_target="tpu_custom_call" | custom-call | flops 786432 | bytes 9437184 | tf_op jit(solution)/shard_map/settle/pallas_call | solution.py:220
  (2 shorter events, 0.0 us)
Async XLA Ops:
  4.8 21.3 %collective-permute-start = (f32[2,6,128,128]{3,2,1,0:T(8,128)}, f32[2,6,128,128]{3,2,1,0:T(8,128)}, u32[]{:S(2)}, u32[]{:S(2)}) collective-permute-start(f32[2,6,128,128]{3,2,1,0:T(8,128)} %get-tuple-element.9), channel_id=1, source_target_pairs={{0,1},{1,2},{2,3},{3,0},{4,5},{5,6},{6,7},{7,4},{8,9},{9,10},{10,1... | collective-permute-start | bytes 2359304 | tf_op jit(solution)/shard_map/ppermute | solution.py:340
  4.9 21.2 %collective-permute-start.1 = (f32[2,6,128,128]{3,2,1,0:T(8,128)}, f32[2,6,128,128]{3,2,1,0:T(8,128)}, u32[]{:S(2)}, u32[]{:S(2)}) collective-permute-start(f32[2,6,128,128]{3,2,1,0:T(8,128)} %get-tuple-element.10), channel_id=1, source_target_pairs={{1,0},{2,1},{3,2},{0,3},{5,4},{6,5},{7,6},{4,7},{9,8},{10,9},{11,1... | collective-permute-start | bytes 2359304 | tf_op jit(solution)/shard_map/ppermute | solution.py:340
  8.1 8.2 %copy-start = (f32[3,2,8,128,128]{4,3,2,1,0:T(8,128)S(1)}, f32[3,2,8,128,128]{4,3,2,1,0:T(8,128)}, u32[]{:S(2)}) copy-start(f32[3,2,8,128,128]{4,3,2,1,0:T(8,128)} %refs_1_.3) | copy-start | bytes 9437188
  8.1 47.2 %all-to-all-start = ((f32[16,6,64,128]{3,2,1,0:T(8,128)}), f32[16,6,64,128]{3,2,1,0:T(8,128)}, u32[]{:S(2)}, u32[]{:S(2)}) async-start(f32[16,6,64,128]{3,2,1,0:T(8,128)} %get-tuple-element.13), calls=%async_computation | async-start | bytes 6291456 | tf_op jit(solution)/shard_map/all_to_all | solution.py:362
  16.3 1.0 copy-start.1
  27.9 1.0 copy-start.2
  28.1 15.1 %collective-permute-start.3 = (f32[2,6,128,128]{3,2,1,0:T(8,128)S(1)}, f32[2,6,128,128]{3,2,1,0:T(8,128)S(1)}, u32[]{:S(2)}, u32[]{:S(2)}) collective-permute-start(f32[2,6,128,128]{3,2,1,0:T(8,128)S(1)} %get-tuple-element.16), channel_id=1, source_target_pairs={{1,0},{2,1},{3,2},{0,3},{5,4},{6,5},{7,6},{4,7},{9,8},{10,9},{11,1... | collective-permute-start | bytes 2359304 | tf_op jit(solution)/shard_map/ppermute | solution.py:340
  28.3 20.8 %collective-permute-start.2 = (f32[2,6,128,128]{3,2,1,0:T(8,128)S(1)}, f32[2,6,128,128]{3,2,1,0:T(8,128)S(1)}, u32[]{:S(2)}, u32[]{:S(2)}) collective-permute-start(f32[2,6,128,128]{3,2,1,0:T(8,128)S(1)} %get-tuple-element.17), channel_id=1, source_target_pairs={{0,1},{1,2},{2,3},{3,0},{4,5},{5,6},{6,7},{7,4},{8,9},{9,10},{10,1... | collective-permute-start | bytes 2359304 | tf_op jit(solution)/shard_map/ppermute | solution.py:340
  51.4 1.4 copy-start.3
  95.4 5.9 %collective-permute-start.6 = (f32[48,128]{1,0:T(8,128)S(1)}, f32[48,128]{1,0:T(8,128)S(1)}, u32[]{:S(2)}, u32[]{:S(2)}) collective-permute-start(f32[48,128]{1,0:T(8,128)S(1)} %gram.1), channel_id=1, source_target_pairs={{0,3},{1,2},{2,1},{3,0},{4,7},{5,6},{6,5},{7,4},{8,11},{9,10},{10,... | collective-permute-start | bytes 73736 | tf_op jit(solution)/shard_map/ppermute | solution.py:346
  97.9 5.3 %collective-permute-start.5 = (f32[48,128]{1,0:T(8,128)S(1)}, f32[48,128]{1,0:T(8,128)S(1)}, u32[]{:S(2)}, u32[]{:S(2)}) collective-permute-start(f32[48,128]{1,0:T(8,128)S(1)} %gram.1), channel_id=1, source_target_pairs={{0,2},{1,3},{2,0},{3,1},{4,6},{5,7},{6,4},{7,5},{8,10},{9,11},{10,... | collective-permute-start | bytes 73736 | tf_op jit(solution)/shard_map/ppermute | solution.py:346
  101.2 2.1 %collective-permute-start.4 = (f32[48,128]{1,0:T(8,128)S(1)}, f32[48,128]{1,0:T(8,128)S(1)}, u32[]{:S(2)}, u32[]{:S(2)}) collective-permute-start(f32[48,128]{1,0:T(8,128)S(1)} %gram.1), channel_id=1, source_target_pairs={{0,1},{1,0},{2,3},{3,2},{4,5},{5,4},{6,7},{7,6},{8,9},{9,8},{10,11... | collective-permute-start | bytes 73736 | tf_op jit(solution)/shard_map/ppermute | solution.py:346

commit v5 on v4

--- a/solution.py
+++ b/solution.py
@@ -260,7 +260,7 @@
     def clear():
         total_ref[...] = jnp.zeros_like(total_ref)
 
-    total = lax.fori_loop(0, segments // 2, one, total_ref[...], unroll=4)
+    total = lax.fori_loop(0, segments // 2, one, total_ref[...], unroll=8)
     total_ref[...] = total
 
     @pl.when(pl.program_id(0) == pl.num_programs(0) - 1)
@@ -310,7 +310,7 @@
         flat_out[pl.ds(j + half, rows, segments), :] = product[:, lanes:]
         return carry
 
-    lax.fori_loop(0, half, one, 0, unroll=4)
+    lax.fori_loop(0, half, one, 0, unroll=16)
 
 
 def project(sums, scale, block_rows):

time: 169 us -> 168 us (level)
  no operation moved by 1% of the time
where the time goes in v5:
time: 168 us; the launch traced here: 167 us
  blocking collectives  94 us (56%)
  Pallas kernels  25.7 us (15%)
  waiting for transfers between devices  25.4 us (15%)
  starting transfers between devices  18.1 us (11%)
  local copies, waits for them, and re-layouts  2.72 us (2%)
    all_to_all x1, blocking collectives, shards(): lax.all_to_all(change.reshape(sent.shape), plane_axes, 0, 0, tiled=True)  42.7 us
    all_to_all x1, blocking collectives, shards(): block_rows = lax.all_to_all(chunks, ('yl',) + plane_axes, 0, 0, tiled=True)  35.4 us
    all_to_all x1, blocking collectives, summed(): return lax.all_to_all(copies, plane_axes, 0, 0, tiled=True)  15.9 us
    ppermute x2, waiting for transfers between devices, exchange(): lax.ppermute(high, ('yh', 'c'), up)  10.6 us
    ppermute x2, waiting for transfers between devices, exchange(): lax.ppermute(low, ('yh', 'c'), down)  10.1 us
    all_to_all x1, starting transfers between devices, shards(): panel_rows = lax.all_to_all(sent, plane_axes, 0, 0, tiled=True)  8.17 us
    pallas_call x2, Pallas kernels, inner(): pl.pallas_call(body, in_specs=[pl.BlockSpec(memory_space=pltpu.SMEM)] + [...  8.07 us
    ppermute x3, starting transfers between devices, summed(): lax.ppermute(partial, ('yh', 'c'), [(i, i ^ step) for i in range(4)])  5.9 us
  transfers between devices with their start and end apart: 8, of which 5 were waited for; matrix products, arithmetic and copies ran while one was open for 0% of the time, Pallas kernels for 7%

profile of v5, /device:TPU:16, one launch (start us, length us, event | category | flops | bytes accessed | tf_op | source)
XLA Modules:
  0.0 167.3 jit_solution(16277702624595544216)
XLA Ops:
  1.3 3.5 %prepare.1 = (f32[16,6,64,128]{3,2,1,0:T(8,128)}, f32[2,6,128,128]{3,2,1,0:T(8,128)}, f32[2,6,128,128]{3,2,1,0:T(8,128)}) custom-call(s32[1]{0:T(128)S(6)} %copy.5.refs_0_.index_ref, f32[3,2,8,128,128]{4,3,2,1,0:T(8,128)} %refs_1_.3), custom_call_target="tpu_custom_call" | custom-call | bytes 6291456 | tf_op jit(solution)/shard_map/prepare/pallas_call | solution.py:199
  4.8 0.1 collective-permute-start
  4.9 3.2 %collective-permute-start.1 = (f32[2,6,128,128]{3,2,1,0:T(8,128)}, f32[2,6,128,128]{3,2,1,0:T(8,128)}, u32[]{:S(2)}, u32[]{:S(2)}) collective-permute-start(f32[2,6,128,128]{3,2,1,0:T(8,128)} %get-tuple-element.10), channel_id=1, source_target_pairs={{1,0},{2,1},{3,2},{0,3},{5,4},{6,5},{7,6},{4,7},{9,8},{10,9},{11,1... | collective-permute-start | bytes 2359304 | tf_op jit(solution)/shard_map/ppermute | solution.py:340
  8.1 0.0 copy-start
  8.1 8.2 %all-to-all-start = ((f32[16,6,64,128]{3,2,1,0:T(8,128)}), f32[16,6,64,128]{3,2,1,0:T(8,128)}, u32[]{:S(2)}, u32[]{:S(2)}) async-start(f32[16,6,64,128]{3,2,1,0:T(8,128)} %get-tuple-element.13), calls=%async_computation | async-start | bytes 6291456 | tf_op jit(solution)/shard_map/all_to_all | solution.py:362
  16.3 0.0 copy-done
  16.3 0.0 copy-start.1
  16.3 1.0 copy-done.1
  17.4 4.0 %inner.2.refs_0_ = f32[2,8,128,128]{3,2,1,0:T(8,128)S(1)} custom-call(s32[1]{0:T(128)S(6)} %copy.5.refs_0_.index_ref, f32[3,2,8,128,128]{4,3,2,1,0:T(8,128)S(1)} %copy-done, f32[8,128,128]{2,1,0:T(8,128)S(1)} %copy-done.1), custom_call_target="tpu_custom_call" | custom-call | flops 13107200 | bytes 3145728 | tf_op jit(solution)/shard_map/inner/pallas_call | solution.py:132
  21.4 4.7 %collective-permute-done.refs_1_ = f32[2,6,128,128]{3,2,1,0:T(8,128)} collective-permute-done((f32[2,6,128,128]{3,2,1,0:T(8,128)}, f32[2,6,128,128]{3,2,1,0:T(8,128)}, u32[]{:S(2)}, u32[]{:S(2)}) %collective-permute-start) | collective-permute-done | bytes 786464 | tf_op jit(solution)/shard_map/ppermute | solution.py:340
  26.1 0.0 collective-permute-done.1.refs_2_
  26.1 1.8 %outer.2.refs_3_ = f32[2,8,128,128]{3,2,1,0:T(8,128)S(1)} custom-call(f32[2,8,128,128]{3,2,1,0:T(8,128)S(1)} %inner.2.refs_0_, f32[2,6,128,128]{3,2,1,0:T(8,128)} %collective-permute-done.refs_1_, f32[2,6,128,128]{3,2,1,0:T(8,128)} %collective-permute-done.1.refs_2_), custom_call_target="tpu_custom_call" | custom-call | flops 26214400000 | bytes 4194304 | tf_op jit(solution)/shard_map/outer/pallas_call | solution.py:159
  27.9 0.0 copy-start.2
  27.9 0.2 fusion
  28.1 0.2 collective-permute-start.3
  28.3 0.5 collective-permute-start.2
  28.8 0.1 copy-done.2
  29.0 4.1 %inner.3.refs_0_ = f32[2,8,128,128]{3,2,1,0:T(8,128)S(1)} custom-call(s32[1]{0:T(128)S(6)} %copy.5.refs_0_.index_ref, f32[3,2,8,128,128]{4,3,2,1,0:T(8,128)S(1)} %copy-done, f32[8,128,128]{2,1,0:T(8,128)S(1)} %copy-done.2, f32[2,8,128,128]{3,2,1,0:T(8,128)S(1)} %outer.2.refs_3_), custom_call_target="tpu_custom_call" | custom-call | flops 13107200 | bytes 3145728 | tf_op jit(solution)/shard_map/inner/pallas_call | solution.py:132
  33.0 10.1 %collective-permute-done.3.refs_2_ = f32[2,6,128,128]{3,2,1,0:T(8,128)S(1)} collective-permute-done((f32[2,6,128,128]{3,2,1,0:T(8,128)S(1)}, f32[2,6,128,128]{3,2,1,0:T(8,128)S(1)}, u32[]{:S(2)}, u32[]{:S(2)}) %collective-permute-start.3) | collective-permute-done | bytes 786464 | tf_op jit(solution)/shard_map/ppermute | solution.py:340
  43.2 5.9 %collective-permute-done.2.refs_1_ = f32[2,6,128,128]{3,2,1,0:T(8,128)S(1)} collective-permute-done((f32[2,6,128,128]{3,2,1,0:T(8,128)S(1)}, f32[2,6,128,128]{3,2,1,0:T(8,128)S(1)}, u32[]{:S(2)}, u32[]{:S(2)}) %collective-permute-start.2) | collective-permute-done | bytes 786464 | tf_op jit(solution)/shard_map/ppermute | solution.py:340
  49.1 2.3 %outer.3 = (f32[2,8,128,128]{3,2,1,0:T(8,128)}, f32[2,16,2,64,128]{4,3,2,1,0:T(8,128)S(1)}) custom-call(f32[2,8,128,128]{3,2,1,0:T(8,128)S(1)} %inner.3.refs_0_, f32[2,6,128,128]{3,2,1,0:T(8,128)S(1)} %collective-permute-done.2.refs_1_, f32[2,6,128,128]{3,2,1,0:T(8,128)S(1)} %collective-permute-done.3.refs_2_), custom_call_target="tpu_custom_call" | custom-call | flops 2621440 | bytes 4194304 | tf_op jit(solution)/shard_map/outer/pallas_call | solution.py:159
  51.4 0.0 copy-start.3
  51.4 1.4 copy-done.3
  52.7 2.6 %all-to-all-done = f32[16,6,64,128]{3,2,1,0:T(8,128)} async-done(((f32[16,6,64,128]{3,2,1,0:T(8,128)}), f32[16,6,64,128]{3,2,1,0:T(8,128)}, u32[]{:S(2)}, u32[]{:S(2)}) %all-to-all-start) | async-done | bytes 3145760 | tf_op jit(solution)/shard_map/all_to_all | solution.py:362
  55.3 35.4 %all_to_all.20 = f32[32,2,64,128]{3,2,1,0:T(8,128)S(1)} all-to-all(f32[32,2,64,128]{3,2,1,0:T(8,128)} %bitcast.10), channel_id=1, replica_groups=mesh['z'=4,'x'=4,'yl'=2,'yh'=2,'c'=2] {'yl','x','z'}, dimensions={0} | all-to-all | bytes 4194304 | tf_op jit(solution)/shard_map/all_to_all | solution.py:371
  90.7 4.3 %gram.1 = f32[48,128]{1,0:T(8,128)S(1)} custom-call(f32[96,64,128]{2,1,0:T(8,128)} %bitcast.1.panel_ref, f32[64,64,128]{2,1,0:T(8,128)S(1)} %bitcast.7), custom_call_target="tpu_custom_call" | custom-call | flops 301989888 | bytes 5242880 | tf_op jit(solution)/shard_map/gram/pallas_call | solution.py:279
  95.0 2.6 %collective-permute-start.6 = (f32[48,128]{1,0:T(8,128)S(1)}, f32[48,128]{1,0:T(8,128)S(1)}, u32[]{:S(2)}, u32[]{:S(2)}) collective-permute-start(f32[48,128]{1,0:T(8,128)S(1)} %gram.1), channel_id=1, source_target_pairs={{0,3},{1,2},{2,1},{3,0},{4,7},{5,6},{6,5},{7,4},{8,11},{9,10},{10,... | collective-permute-start | bytes 73736 | tf_op jit(solution)/shard_map/ppermute | solution.py:346
  97.6 3.3 %collective-permute-start.5 = (f32[48,128]{1,0:T(8,128)S(1)}, f32[48,128]{1,0:T(8,128)S(1)}, u32[]{:S(2)}, u32[]{:S(2)}) collective-permute-start(f32[48,128]{1,0:T(8,128)S(1)} %gram.1), channel_id=1, source_target_pairs={{0,2},{1,3},{2,0},{3,1},{4,6},{5,7},{6,4},{7,5},{8,10},{9,11},{10,... | collective-permute-start | bytes 73736 | tf_op jit(solution)/shard_map/ppermute | solution.py:346
  100.9 0.0 collective-permute-start.4
  100.9 0.0 collective-permute-done.6
  100.9 2.0 %collective-permute-done.5 = f32[48,128]{1,0:T(8,128)S(1)} collective-permute-done((f32[48,128]{1,0:T(8,128)S(1)}, f32[48,128]{1,0:T(8,128)S(1)}, u32[]{:S(2)}, u32[]{:S(2)}) %collective-permute-start.5) | collective-permute-done | bytes 24608 | tf_op jit(solution)/shard_map/ppermute | solution.py:346
  102.9 0.0 collective-permute-done.4
  103.0 15.9 %all_to_all.21.refs_0_ = f32[16,48,128]{2,1,0:T(8,128)S(1)} all-to-all(f32[16,48,128]{2,1,0:T(8,128)S(1)} %broadcast_in_dim.2), channel_id=1, replica_groups=mesh['z'=4,'x'=4,'yl'=2,'yh'=2,'c'=2] {'x','z'}, dimensions={0} | all-to-all | bytes 786432 | tf_op jit(solution)/shard_map/all_to_all | solution.py:349
  118.9 3.6 %project.1 = f32[96,64,128]{2,1,0:T(8,128)S(1)} custom-call(f32[16,48,128]{2,1,0:T(8,128)S(1)} %all_to_all.21.refs_0_, f32[64,64,128]{2,1,0:T(8,128)S(1)} %bitcast.8), custom_call_target="tpu_custom_call" | custom-call | flops 301989888 | bytes 5242880 | tf_op jit(solution)/shard_map/project/pallas_call | solution.py:323
  122.5 42.7 %all_to_all.22.change_ref = f32[16,6,64,128]{3,2,1,0:T(8,128)S(1)} all-to-all(f32[16,6,64,128]{3,2,1,0:T(8,128)S(1)} %bitcast.9), channel_id=1, replica_groups=mesh['z'=4,'x'=4,'yl'=2,'yh'=2,'c'=2] {'x','z'}, dimensions={0} | all-to-all | bytes 6291456 | tf_op jit(solution)/shard_map/all_to_all | solution.py:378
  165.2 2.0 %settle.1 = f32[6,16,64,128]{3,2,1,0:T(8,128)} custom-call(f32[6,16,64,128]{3,2,1,0:T(8,128)S(1)} %bitcast.6, f32[16,6,64,128]{3,2,1,0:T(8,128)S(1)} %all_to_all.22.change_ref), custom_call_target="tpu_custom_call" | custom-call | flops 786432 | bytes 9437184 | tf_op jit(solution)/shard_map/settle/pallas_call | solution.py:220
  (2 shorter events, 0.0 us)
Async XLA Ops:
  4.8 21.3 %collective-permute-start = (f32[2,6,128,128]{3,2,1,0:T(8,128)}, f32[2,6,128,128]{3,2,1,0:T(8,128)}, u32[]{:S(2)}, u32[]{:S(2)}) collective-permute-start(f32[2,6,128,128]{3,2,1,0:T(8,128)} %get-tuple-element.9), channel_id=1, source_target_pairs={{0,1},{1,2},{2,3},{3,0},{4,5},{5,6},{6,7},{7,4},{8,9},{9,10},{10,1... | collective-permute-start | bytes 2359304 | tf_op jit(solution)/shard_map/ppermute | solution.py:340
  4.9 21.2 %collective-permute-start.1 = (f32[2,6,128,128]{3,2,1,0:T(8,128)}, f32[2,6,128,128]{3,2,1,0:T(8,128)}, u32[]{:S(2)}, u32[]{:S(2)}) collective-permute-start(f32[2,6,128,128]{3,2,1,0:T(8,128)} %get-tuple-element.10), channel_id=1, source_target_pairs={{1,0},{2,1},{3,2},{0,3},{5,4},{6,5},{7,6},{4,7},{9,8},{10,9},{11,1... | collective-permute-start | bytes 2359304 | tf_op jit(solution)/shard_map/ppermute | solution.py:340
  8.1 8.2 %copy-start = (f32[3,2,8,128,128]{4,3,2,1,0:T(8,128)S(1)}, f32[3,2,8,128,128]{4,3,2,1,0:T(8,128)}, u32[]{:S(2)}) copy-start(f32[3,2,8,128,128]{4,3,2,1,0:T(8,128)} %refs_1_.3) | copy-start | bytes 9437188
  8.1 47.2 %all-to-all-start = ((f32[16,6,64,128]{3,2,1,0:T(8,128)}), f32[16,6,64,128]{3,2,1,0:T(8,128)}, u32[]{:S(2)}, u32[]{:S(2)}) async-start(f32[16,6,64,128]{3,2,1,0:T(8,128)} %get-tuple-element.13), calls=%async_computation | async-start | bytes 6291456 | tf_op jit(solution)/shard_map/all_to_all | solution.py:362
  16.3 1.0 copy-start.1
  27.9 1.0 copy-start.2
  28.1 15.1 %collective-permute-start.3 = (f32[2,6,128,128]{3,2,1,0:T(8,128)S(1)}, f32[2,6,128,128]{3,2,1,0:T(8,128)S(1)}, u32[]{:S(2)}, u32[]{:S(2)}) collective-permute-start(f32[2,6,128,128]{3,2,1,0:T(8,128)S(1)} %get-tuple-element.16), channel_id=1, source_target_pairs={{1,0},{2,1},{3,2},{0,3},{5,4},{6,5},{7,6},{4,7},{9,8},{10,9},{11,1... | collective-permute-start | bytes 2359304 | tf_op jit(solution)/shard_map/ppermute | solution.py:340
  28.3 20.8 %collective-permute-start.2 = (f32[2,6,128,128]{3,2,1,0:T(8,128)S(1)}, f32[2,6,128,128]{3,2,1,0:T(8,128)S(1)}, u32[]{:S(2)}, u32[]{:S(2)}) collective-permute-start(f32[2,6,128,128]{3,2,1,0:T(8,128)S(1)} %get-tuple-element.17), channel_id=1, source_target_pairs={{0,1},{1,2},{2,3},{3,0},{4,5},{5,6},{6,7},{7,4},{8,9},{9,10},{10,1... | collective-permute-start | bytes 2359304 | tf_op jit(solution)/shard_map/ppermute | solution.py:340
  51.4 1.4 copy-start.3
  95.0 5.9 %collective-permute-start.6 = (f32[48,128]{1,0:T(8,128)S(1)}, f32[48,128]{1,0:T(8,128)S(1)}, u32[]{:S(2)}, u32[]{:S(2)}) collective-permute-start(f32[48,128]{1,0:T(8,128)S(1)} %gram.1), channel_id=1, source_target_pairs={{0,3},{1,2},{2,1},{3,0},{4,7},{5,6},{6,5},{7,4},{8,11},{9,10},{10,... | collective-permute-start | bytes 73736 | tf_op jit(solution)/shard_map/ppermute | solution.py:346
  97.6 5.3 %collective-permute-start.5 = (f32[48,128]{1,0:T(8,128)S(1)}, f32[48,128]{1,0:T(8,128)S(1)}, u32[]{:S(2)}, u32[]{:S(2)}) collective-permute-start(f32[48,128]{1,0:T(8,128)S(1)} %gram.1), channel_id=1, source_target_pairs={{0,2},{1,3},{2,0},{3,1},{4,6},{5,7},{6,4},{7,5},{8,10},{9,11},{10,... | collective-permute-start | bytes 73736 | tf_op jit(solution)/shard_map/ppermute | solution.py:346
  100.9 2.1 %collective-permute-start.4 = (f32[48,128]{1,0:T(8,128)S(1)}, f32[48,128]{1,0:T(8,128)S(1)}, u32[]{:S(2)}, u32[]{:S(2)}) collective-permute-start(f32[48,128]{1,0:T(8,128)S(1)} %gram.1), channel_id=1, source_target_pairs={{0,1},{1,0},{2,3},{3,2},{4,5},{5,4},{6,7},{7,6},{8,9},{9,8},{10,11... | collective-permute-start | bytes 73736 | tf_op jit(solution)/shard_map/ppermute | solution.py:346

commit v6 on v5

--- a/solution.py
+++ b/solution.py
@@ -102,11 +102,11 @@
         lax.fori_loop(0, rows // strip, one, 0)
         moves = [(held.at[b], out_ref.at[b])]
         if second:
-            copies, spots, _, height, _ = chunk_ref.shape
-            source = held.at[b].reshape(spots, height, columns)
-            moves += [(source, chunk_ref.at[j, :, b]) for j in range(copies)]
+            copies, depth, width, _, height, _ = chunk_ref.shape
+            source = held.at[b].reshape(width, depth, height, columns)
+            moves += [(source.at[x], chunk_ref.at[j, :, x, b]) for j in range(copies) for x in range(width)]
         for i, move in enumerate(moves):
-            copy = pltpu.make_async_copy(*move, sems.at[3 * bands + 3 * b + i])
+            copy = pltpu.make_async_copy(*move, sems.at[3 * bands + len(moves) * b + i])
             copy.start()
             leaving.append(copy)
     for copy in leaving:
@@ -149,8 +149,8 @@
     weight = 10 if second else OUTER_WEIGHT
     out_shape = [jax.ShapeDtypeStruct(part.shape, jnp.float32)]
     if second:
-        copies, spots = chunks
-        out_shape.append(jax.ShapeDtypeStruct((copies, spots, bands, planes * rows // spots, columns), jnp.float32))
+        height = planes * rows // (chunks[1] * chunks[2])
+        out_shape.append(jax.ShapeDtypeStruct(chunks + (bands, height, columns), jnp.float32))
     halo = pltpu.VMEM((bands, reach, rows, columns), jnp.float32)
 
     def body(*refs):
@@ -161,7 +161,7 @@
         in_specs=[hbm] * 3,
         out_specs=[hbm] * len(out_shape),
         out_shape=out_shape,
-        scratch_shapes=[pltpu.VMEM(part.shape, jnp.float32), halo, halo, pltpu.SemaphoreType.DMA((6 * bands,))],
+        scratch_shapes=[pltpu.VMEM(part.shape, jnp.float32), halo, halo, pltpu.SemaphoreType.DMA((12 * bands,))],
         compiler_params=pltpu.CompilerParams(vmem_limit_bytes=vmem_bytes),
         cost_estimate=pl.CostEstimate(flops=weight * part.size, bytes_accessed=16 * part.size, transcendentals=0),
         name="outer",
@@ -365,11 +365,11 @@
     (first,) = outer(inner(block_index, panels, potential), before, after)
     before, after = exchange(first[:, :reach], first[:, planes - reach :])
     part = inner(block_index, panels, potential, first)
-    filtered, chunks = outer(part, before, after, (lax.axis_size("yl"), spots))
+    filtered, chunks = outer(part, before, after, tuple(lax.axis_size(axis) for axis in ("yl", "z", "x")))
     chunks, panel_rows = lax.optimization_barrier((chunks, panel_rows))
-    chunks = chunks.reshape((-1,) + chunks.shape[2:])
+    chunks = chunks.reshape((-1,) + chunks.shape[3:])
     block_rows = lax.all_to_all(
-        chunks, ("yl",) + plane_axes, 0, 0, tiled=True
+        chunks, ("yl", "z", "x"), 0, 0, tiled=True
     )
     block_rows = block_rows.reshape((-1,) + chunks.shape[2:])
 

time: 168 us -> 168 us (level)
  transfers between devices with their start and end apart: 8 -> 8, of which waited for: 5 -> 5; matrix products, arithmetic and copies ran while one was open for 0% -> 0% of each run, Pallas kernels for 7% -> 8%
where the time goes in v6:
time: 168 us; the launch traced here: 167 us
  blocking collectives  94.5 us (56%)
  Pallas kernels  26.2 us (16%)
  waiting for transfers between devices  24.9 us (15%)
  starting transfers between devices  17.7 us (11%)
  local copies, waits for them, and re-layouts  2.72 us (2%)
    all_to_all x1, blocking collectives, shards(): lax.all_to_all(change.reshape(sent.shape), plane_axes, 0, 0, tiled=True)  42.7 us
    all_to_all x1, blocking collectives, shards(): block_rows = lax.all_to_all(chunks, ('yl', 'z', 'x'), 0, 0, tiled=True)  35.9 us
    all_to_all x1, blocking collectives, summed(): return lax.all_to_all(copies, plane_axes, 0, 0, tiled=True)  15.9 us
    ppermute x2, waiting for transfers between devices, exchange(): lax.ppermute(high, ('yh', 'c'), up)  10.6 us
    ppermute x2, waiting for transfers between devices, exchange(): lax.ppermute(low, ('yh', 'c'), down)  10.1 us
    all_to_all x1, starting transfers between devices, shards(): panel_rows = lax.all_to_all(sent, plane_axes, 0, 0, tiled=True)  8.17 us
    pallas_call x2, Pallas kernels, inner(): pl.pallas_call(body, in_specs=[pl.BlockSpec(memory_space=pltpu.SMEM)] + [...  8.07 us
    ppermute x3, starting transfers between devices, summed(): lax.ppermute(partial, ('yh', 'c'), [(i, i ^ step) for i in range(4)])  5.49 us
  transfers between devices with their start and end apart: 8, of which 5 were waited for; matrix products, arithmetic and copies ran while one was open for 0% of the time, Pallas kernels for 8%

profile of v6, /device:TPU:16, one launch (start us, length us, event | category | flops | bytes accessed | tf_op | source)
XLA Modules:
  0.0 167.4 jit_solution(6745370718298611071)
XLA Ops:
  1.3 3.5 %prepare.1 = (f32[16,6,64,128]{3,2,1,0:T(8,128)}, f32[2,6,128,128]{3,2,1,0:T(8,128)}, f32[2,6,128,128]{3,2,1,0:T(8,128)}) custom-call(s32[1]{0:T(128)S(6)} %copy.5.refs_0_.index_ref, f32[3,2,8,128,128]{4,3,2,1,0:T(8,128)} %refs_1_.3), custom_call_target="tpu_custom_call" | custom-call | bytes 6291456 | tf_op jit(solution)/shard_map/prepare/pallas_call | solution.py:199
  4.8 0.1 collective-permute-start
  4.9 3.2 %collective-permute-start.1 = (f32[2,6,128,128]{3,2,1,0:T(8,128)}, f32[2,6,128,128]{3,2,1,0:T(8,128)}, u32[]{:S(2)}, u32[]{:S(2)}) collective-permute-start(f32[2,6,128,128]{3,2,1,0:T(8,128)} %get-tuple-element.10), channel_id=1, source_target_pairs={{1,0},{2,1},{3,2},{0,3},{5,4},{6,5},{7,6},{4,7},{9,8},{10,9},{11,1... | collective-permute-start | bytes 2359304 | tf_op jit(solution)/shard_map/ppermute | solution.py:340
  8.1 0.0 copy-start
  8.1 8.2 %all-to-all-start = ((f32[16,6,64,128]{3,2,1,0:T(8,128)}), f32[16,6,64,128]{3,2,1,0:T(8,128)}, u32[]{:S(2)}, u32[]{:S(2)}) async-start(f32[16,6,64,128]{3,2,1,0:T(8,128)} %get-tuple-element.13), calls=%async_computation | async-start | bytes 6291456 | tf_op jit(solution)/shard_map/all_to_all | solution.py:362
  16.3 0.0 copy-done
  16.3 0.0 copy-start.1
  16.3 1.0 copy-done.1
  17.4 4.0 %inner.2.refs_0_ = f32[2,8,128,128]{3,2,1,0:T(8,128)S(1)} custom-call(s32[1]{0:T(128)S(6)} %copy.5.refs_0_.index_ref, f32[3,2,8,128,128]{4,3,2,1,0:T(8,128)S(1)} %copy-done, f32[8,128,128]{2,1,0:T(8,128)S(1)} %copy-done.1), custom_call_target="tpu_custom_call" | custom-call | flops 13107200 | bytes 3145728 | tf_op jit(solution)/shard_map/inner/pallas_call | solution.py:132
  21.4 4.7 %collective-permute-done.refs_1_ = f32[2,6,128,128]{3,2,1,0:T(8,128)} collective-permute-done((f32[2,6,128,128]{3,2,1,0:T(8,128)}, f32[2,6,128,128]{3,2,1,0:T(8,128)}, u32[]{:S(2)}, u32[]{:S(2)}) %collective-permute-start) | collective-permute-done | bytes 786464 | tf_op jit(solution)/shard_map/ppermute | solution.py:340
  26.1 0.0 collective-permute-done.1.refs_2_
  26.1 1.9 %outer.2.refs_3_ = f32[2,8,128,128]{3,2,1,0:T(8,128)S(1)} custom-call(f32[2,8,128,128]{3,2,1,0:T(8,128)S(1)} %inner.2.refs_0_, f32[2,6,128,128]{3,2,1,0:T(8,128)} %collective-permute-done.refs_1_, f32[2,6,128,128]{3,2,1,0:T(8,128)} %collective-permute-done.1.refs_2_), custom_call_target="tpu_custom_call" | custom-call | flops 26214400000 | bytes 4194304 | tf_op jit(solution)/shard_map/outer/pallas_call | solution.py:159
  28.0 0.0 copy-start.2
  28.0 0.2 fusion
  28.2 0.2 collective-permute-start.3
  28.4 0.5 collective-permute-start.2
  28.9 0.1 copy-done.2
  29.1 4.1 %inner.3.refs_0_ = f32[2,8,128,128]{3,2,1,0:T(8,128)S(1)} custom-call(s32[1]{0:T(128)S(6)} %copy.5.refs_0_.index_ref, f32[3,2,8,128,128]{4,3,2,1,0:T(8,128)S(1)} %copy-done, f32[8,128,128]{2,1,0:T(8,128)S(1)} %copy-done.2, f32[2,8,128,128]{3,2,1,0:T(8,128)S(1)} %outer.2.refs_3_), custom_call_target="tpu_custom_call" | custom-call | flops 13107200 | bytes 3145728 | tf_op jit(solution)/shard_map/inner/pallas_call | solution.py:132
  33.1 10.1 %collective-permute-done.3.refs_2_ = f32[2,6,128,128]{3,2,1,0:T(8,128)S(1)} collective-permute-done((f32[2,6,128,128]{3,2,1,0:T(8,128)S(1)}, f32[2,6,128,128]{3,2,1,0:T(8,128)S(1)}, u32[]{:S(2)}, u32[]{:S(2)}) %collective-permute-start.3) | collective-permute-done | bytes 786464 | tf_op jit(solution)/shard_map/ppermute | solution.py:340
  43.3 5.9 %collective-permute-done.2.refs_1_ = f32[2,6,128,128]{3,2,1,0:T(8,128)S(1)} collective-permute-done((f32[2,6,128,128]{3,2,1,0:T(8,128)S(1)}, f32[2,6,128,128]{3,2,1,0:T(8,128)S(1)}, u32[]{:S(2)}, u32[]{:S(2)}) %collective-permute-start.2) | collective-permute-done | bytes 786464 | tf_op jit(solution)/shard_map/ppermute | solution.py:340
  49.2 2.7 %outer.3 = (f32[2,8,128,128]{3,2,1,0:T(8,128)}, f32[2,4,4,2,64,128]{5,4,3,2,1,0:T(8,128)S(1)}) custom-call(f32[2,8,128,128]{3,2,1,0:T(8,128)S(1)} %inner.3.refs_0_, f32[2,6,128,128]{3,2,1,0:T(8,128)S(1)} %collective-permute-done.2.refs_1_, f32[2,6,128,128]{3,2,1,0:T(8,128)S(1)} %collective-permute-done.3.refs_2_), custom_call_target="tpu_custom_call" | custom-call | flops 2621440 | bytes 4194304 | tf_op jit(solution)/shard_map/outer/pallas_call | solution.py:159
  51.9 0.0 copy-start.3
  51.9 1.4 copy-done.3
  53.2 2.1 %all-to-all-done = f32[16,6,64,128]{3,2,1,0:T(8,128)} async-done(((f32[16,6,64,128]{3,2,1,0:T(8,128)}), f32[16,6,64,128]{3,2,1,0:T(8,128)}, u32[]{:S(2)}, u32[]{:S(2)}) %all-to-all-start) | async-done | bytes 3145760 | tf_op jit(solution)/shard_map/all_to_all | solution.py:362
  55.3 35.9 %all_to_all.20 = f32[32,2,64,128]{3,2,1,0:T(8,128)S(1)} all-to-all(f32[32,2,64,128]{3,2,1,0:T(8,128)} %bitcast.10), channel_id=1, replica_groups=mesh['z'=4,'x'=4,'yl'=2,'yh'=2,'c'=2] {'yl','z','x'}, dimensions={0} | all-to-all | bytes 4194304 | tf_op jit(solution)/shard_map/all_to_all | solution.py:371
  91.3 4.3 %gram.1 = f32[48,128]{1,0:T(8,128)S(1)} custom-call(f32[96,64,128]{2,1,0:T(8,128)} %bitcast.1.panel_ref, f32[64,64,128]{2,1,0:T(8,128)S(1)} %bitcast.7), custom_call_target="tpu_custom_call" | custom-call | flops 301989888 | bytes 5242880 | tf_op jit(solution)/shard_map/gram/pallas_call | solution.py:279
  95.6 2.2 %collective-permute-start.6 = (f32[48,128]{1,0:T(8,128)S(1)}, f32[48,128]{1,0:T(8,128)S(1)}, u32[]{:S(2)}, u32[]{:S(2)}) collective-permute-start(f32[48,128]{1,0:T(8,128)S(1)} %gram.1), channel_id=1, source_target_pairs={{0,3},{1,2},{2,1},{3,0},{4,7},{5,6},{6,5},{7,4},{8,11},{9,10},{10,... | collective-permute-start | bytes 73736 | tf_op jit(solution)/shard_map/ppermute | solution.py:346
  97.7 3.3 %collective-permute-start.5 = (f32[48,128]{1,0:T(8,128)S(1)}, f32[48,128]{1,0:T(8,128)S(1)}, u32[]{:S(2)}, u32[]{:S(2)}) collective-permute-start(f32[48,128]{1,0:T(8,128)S(1)} %gram.1), channel_id=1, source_target_pairs={{0,2},{1,3},{2,0},{3,1},{4,6},{5,7},{6,4},{7,5},{8,10},{9,11},{10,... | collective-permute-start | bytes 73736 | tf_op jit(solution)/shard_map/ppermute | solution.py:346
  101.0 0.0 collective-permute-start.4
  101.0 0.0 collective-permute-done.6
  101.0 2.0 %collective-permute-done.5 = f32[48,128]{1,0:T(8,128)S(1)} collective-permute-done((f32[48,128]{1,0:T(8,128)S(1)}, f32[48,128]{1,0:T(8,128)S(1)}, u32[]{:S(2)}, u32[]{:S(2)}) %collective-permute-start.5) | collective-permute-done | bytes 24608 | tf_op jit(solution)/shard_map/ppermute | solution.py:346
  103.1 0.0 collective-permute-done.4
  103.1 15.9 %all_to_all.21.refs_0_ = f32[16,48,128]{2,1,0:T(8,128)S(1)} all-to-all(f32[16,48,128]{2,1,0:T(8,128)S(1)} %broadcast_in_dim.2), channel_id=1, replica_groups=mesh['z'=4,'x'=4,'yl'=2,'yh'=2,'c'=2] {'x','z'}, dimensions={0} | all-to-all | bytes 786432 | tf_op jit(solution)/shard_map/all_to_all | solution.py:349
  119.0 3.6 %project.1 = f32[96,64,128]{2,1,0:T(8,128)S(1)} custom-call(f32[16,48,128]{2,1,0:T(8,128)S(1)} %all_to_all.21.refs_0_, f32[64,64,128]{2,1,0:T(8,128)S(1)} %bitcast.8), custom_call_target="tpu_custom_call" | custom-call | flops 301989888 | bytes 5242880 | tf_op jit(solution)/shard_map/project/pallas_call | solution.py:323
  122.6 42.7 %all_to_all.22.change_ref = f32[16,6,64,128]{3,2,1,0:T(8,128)S(1)} all-to-all(f32[16,6,64,128]{3,2,1,0:T(8,128)S(1)} %bitcast.9), channel_id=1, replica_groups=mesh['z'=4,'x'=4,'yl'=2,'yh'=2,'c'=2] {'x','z'}, dimensions={0} | all-to-all | bytes 6291456 | tf_op jit(solution)/shard_map/all_to_all | solution.py:378
  165.4 2.0 %settle.1 = f32[6,16,64,128]{3,2,1,0:T(8,128)} custom-call(f32[6,16,64,128]{3,2,1,0:T(8,128)S(1)} %bitcast.6, f32[16,6,64,128]{3,2,1,0:T(8,128)S(1)} %all_to_all.22.change_ref), custom_call_target="tpu_custom_call" | custom-call | flops 786432 | bytes 9437184 | tf_op jit(solution)/shard_map/settle/pallas_call | solution.py:220
  (2 shorter events, 0.0 us)
Async XLA Ops:
  4.8 21.3 %collective-permute-start = (f32[2,6,128,128]{3,2,1,0:T(8,128)}, f32[2,6,128,128]{3,2,1,0:T(8,128)}, u32[]{:S(2)}, u32[]{:S(2)}) collective-permute-start(f32[2,6,128,128]{3,2,1,0:T(8,128)} %get-tuple-element.9), channel_id=1, source_target_pairs={{0,1},{1,2},{2,3},{3,0},{4,5},{5,6},{6,7},{7,4},{8,9},{9,10},{10,1... | collective-permute-start | bytes 2359304 | tf_op jit(solution)/shard_map/ppermute | solution.py:340
  4.9 21.2 %collective-permute-start.1 = (f32[2,6,128,128]{3,2,1,0:T(8,128)}, f32[2,6,128,128]{3,2,1,0:T(8,128)}, u32[]{:S(2)}, u32[]{:S(2)}) collective-permute-start(f32[2,6,128,128]{3,2,1,0:T(8,128)} %get-tuple-element.10), channel_id=1, source_target_pairs={{1,0},{2,1},{3,2},{0,3},{5,4},{6,5},{7,6},{4,7},{9,8},{10,9},{11,1... | collective-permute-start | bytes 2359304 | tf_op jit(solution)/shard_map/ppermute | solution.py:340
  8.1 8.2 %copy-start = (f32[3,2,8,128,128]{4,3,2,1,0:T(8,128)S(1)}, f32[3,2,8,128,128]{4,3,2,1,0:T(8,128)}, u32[]{:S(2)}) copy-start(f32[3,2,8,128,128]{4,3,2,1,0:T(8,128)} %refs_1_.3) | copy-start | bytes 9437188
  8.1 47.2 %all-to-all-start = ((f32[16,6,64,128]{3,2,1,0:T(8,128)}), f32[16,6,64,128]{3,2,1,0:T(8,128)}, u32[]{:S(2)}, u32[]{:S(2)}) async-start(f32[16,6,64,128]{3,2,1,0:T(8,128)} %get-tuple-element.13), calls=%async_computation | async-start | bytes 6291456 | tf_op jit(solution)/shard_map/all_to_all | solution.py:362
  16.3 1.0 copy-start.1
  28.0 1.0 copy-start.2
  28.2 15.1 %collective-permute-start.3 = (f32[2,6,128,128]{3,2,1,0:T(8,128)S(1)}, f32[2,6,128,128]{3,2,1,0:T(8,128)S(1)}, u32[]{:S(2)}, u32[]{:S(2)}) collective-permute-start(f32[2,6,128,128]{3,2,1,0:T(8,128)S(1)} %get-tuple-element.16), channel_id=1, source_target_pairs={{1,0},{2,1},{3,2},{0,3},{5,4},{6,5},{7,6},{4,7},{9,8},{10,9},{11,1... | collective-permute-start | bytes 2359304 | tf_op jit(solution)/shard_map/ppermute | solution.py:340
  28.4 20.8 %collective-permute-start.2 = (f32[2,6,128,128]{3,2,1,0:T(8,128)S(1)}, f32[2,6,128,128]{3,2,1,0:T(8,128)S(1)}, u32[]{:S(2)}, u32[]{:S(2)}) collective-permute-start(f32[2,6,128,128]{3,2,1,0:T(8,128)S(1)} %get-tuple-element.17), channel_id=1, source_target_pairs={{0,1},{1,2},{2,3},{3,0},{4,5},{5,6},{6,7},{7,4},{8,9},{9,10},{10,1... | collective-permute-start | bytes 2359304 | tf_op jit(solution)/shard_map/ppermute | solution.py:340
  51.9 1.4 copy-start.3
  95.6 5.5 %collective-permute-start.6 = (f32[48,128]{1,0:T(8,128)S(1)}, f32[48,128]{1,0:T(8,128)S(1)}, u32[]{:S(2)}, u32[]{:S(2)}) collective-permute-start(f32[48,128]{1,0:T(8,128)S(1)} %gram.1), channel_id=1, source_target_pairs={{0,3},{1,2},{2,1},{3,0},{4,7},{5,6},{6,5},{7,4},{8,11},{9,10},{10,... | collective-permute-start | bytes 73736 | tf_op jit(solution)/shard_map/ppermute | solution.py:346
  97.7 5.3 %collective-permute-start.5 = (f32[48,128]{1,0:T(8,128)S(1)}, f32[48,128]{1,0:T(8,128)S(1)}, u32[]{:S(2)}, u32[]{:S(2)}) collective-permute-start(f32[48,128]{1,0:T(8,128)S(1)} %gram.1), channel_id=1, source_target_pairs={{0,2},{1,3},{2,0},{3,1},{4,6},{5,7},{6,4},{7,5},{8,10},{9,11},{10,... | collective-permute-start | bytes 73736 | tf_op jit(solution)/shard_map/ppermute | solution.py:346
  101.0 2.0 %collective-permute-start.4 = (f32[48,128]{1,0:T(8,128)S(1)}, f32[48,128]{1,0:T(8,128)S(1)}, u32[]{:S(2)}, u32[]{:S(2)}) collective-permute-start(f32[48,128]{1,0:T(8,128)S(1)} %gram.1), channel_id=1, source_target_pairs={{0,1},{1,0},{2,3},{3,2},{4,5},{5,4},{6,7},{7,6},{8,9},{9,8},{10,11... | collective-permute-start | bytes 73736 | tf_op jit(solution)/shard_map/ppermute | solution.py:346

commit v7 on v6

--- a/solution.py
+++ b/solution.py
@@ -208,21 +208,28 @@
     )(index, panels)
 
 
-def settle_kernel(panel_ref, change_ref, out_ref):
-    for i in range(change_ref.shape[0]):
-        out_ref[:, i] = panel_ref[:, i] - change_ref[i]
+def settle_kernel(panel_ref, change_ref, out_ref, held, sems):
+    spots = change_ref.shape[0]
+    step = spots // 4
+    leaving = []
+    for part in range(4):
+        for i in range(part * step, (part + 1) * step):
+            held[:, i] = panel_ref[:, i] - change_ref[i]
+        place = pl.ds(part * step, step)
+        leaving.append(pltpu.make_async_copy(held.at[:, place], out_ref.at[:, place], sems.at[part]))
+        leaving[part].start()
+    for copy in leaving:
+        copy.wait()
 
 
 def settle(rows, change):
-    count, spots = rows.shape[:2]
-    step = spots // 2
-    mine = pl.BlockSpec((count, step) + rows.shape[2:], lambda i: (0, i, 0, 0))
+    whole = pl.BlockSpec(memory_space=pltpu.VMEM)
     return pl.pallas_call(
         settle_kernel,
-        grid=(spots // step,),
-        in_specs=[mine, pl.BlockSpec((step, count) + rows.shape[2:], lambda i: (i, 0, 0, 0))],
-        out_specs=mine,
+        in_specs=[whole, whole],
+        out_specs=hbm,
         out_shape=jax.ShapeDtypeStruct(rows.shape, jnp.float32),
+        scratch_shapes=[pltpu.VMEM(rows.shape, jnp.float32), pltpu.SemaphoreType.DMA((4,))],
         compiler_params=pltpu.CompilerParams(vmem_limit_bytes=vmem_bytes),
         cost_estimate=pl.CostEstimate(flops=rows.size, bytes_accessed=12 * rows.size, transcendentals=0),
         name="settle",

time: 168 us -> 168 us (level)
  no operation moved by 1% of the time
where the time goes in v7:
time: 168 us; the launch traced here: 167 us
  blocking collectives  94.5 us (56%)
  Pallas kernels  25.9 us (15%)
  waiting for transfers between devices  24.9 us (15%)
  starting transfers between devices  17.7 us (11%)
  local copies, waits for them, and re-layouts  2.72 us (2%)
    all_to_all x1, blocking collectives, shards(): lax.all_to_all(change.reshape(sent.shape), plane_axes, 0, 0, tiled=True)  42.7 us
    all_to_all x1, blocking collectives, shards(): block_rows = lax.all_to_all(chunks, ('yl', 'z', 'x'), 0, 0, tiled=True)  35.9 us
    all_to_all x1, blocking collectives, summed(): return lax.all_to_all(copies, plane_axes, 0, 0, tiled=True)  15.9 us
    ppermute x2, waiting for transfers between devices, exchange(): lax.ppermute(high, ('yh', 'c'), up)  10.6 us
    ppermute x2, waiting for transfers between devices, exchange(): lax.ppermute(low, ('yh', 'c'), down)  10.1 us
    all_to_all x1, starting transfers between devices, shards(): panel_rows = lax.all_to_all(sent, plane_axes, 0, 0, tiled=True)  8.17 us
    pallas_call x2, Pallas kernels, inner(): pl.pallas_call(body, in_specs=[pl.BlockSpec(memory_space=pltpu.SMEM)] + [...  8.07 us
    ppermute x3, starting transfers between devices, summed(): lax.ppermute(partial, ('yh', 'c'), [(i, i ^ step) for i in range(4)])  5.49 us
  transfers between devices with their start and end apart: 8, of which 5 were waited for; matrix products, arithmetic and copies ran while one was open for 0% of the time, Pallas kernels for 8%

profile of v7, /device:TPU:16, one launch (start us, length us, event | category | flops | bytes accessed | tf_op | source)
XLA Modules:
  0.0 167.3 jit_solution(1462976672502711696)
XLA Ops:
  1.3 3.5 %prepare.1 = (f32[16,6,64,128]{3,2,1,0:T(8,128)}, f32[2,6,128,128]{3,2,1,0:T(8,128)}, f32[2,6,128,128]{3,2,1,0:T(8,128)}) custom-call(s32[1]{0:T(128)S(6)} %copy.5.refs_0_.index_ref, f32[3,2,8,128,128]{4,3,2,1,0:T(8,128)} %refs_1_.3), custom_call_target="tpu_custom_call" | custom-call | bytes 6291456 | tf_op jit(solution)/shard_map/prepare/pallas_call | solution.py:199
  4.8 0.1 collective-permute-start
  4.9 3.2 %collective-permute-start.1 = (f32[2,6,128,128]{3,2,1,0:T(8,128)}, f32[2,6,128,128]{3,2,1,0:T(8,128)}, u32[]{:S(2)}, u32[]{:S(2)}) collective-permute-start(f32[2,6,128,128]{3,2,1,0:T(8,128)} %get-tuple-element.10), channel_id=1, source_target_pairs={{1,0},{2,1},{3,2},{0,3},{5,4},{6,5},{7,6},{4,7},{9,8},{10,9},{11,1... | collective-permute-start | bytes 2359304 | tf_op jit(solution)/shard_map/ppermute | solution.py:347
  8.1 0.0 copy-start
  8.1 8.2 %all-to-all-start = ((f32[16,6,64,128]{3,2,1,0:T(8,128)}), f32[16,6,64,128]{3,2,1,0:T(8,128)}, u32[]{:S(2)}, u32[]{:S(2)}) async-start(f32[16,6,64,128]{3,2,1,0:T(8,128)} %get-tuple-element.13), calls=%async_computation | async-start | bytes 6291456 | tf_op jit(solution)/shard_map/all_to_all | solution.py:369
  16.3 0.0 copy-done
  16.3 0.0 copy-start.1
  16.3 1.0 copy-done.1
  17.4 4.0 %inner.2.refs_0_ = f32[2,8,128,128]{3,2,1,0:T(8,128)S(1)} custom-call(s32[1]{0:T(128)S(6)} %copy.5.refs_0_.index_ref, f32[3,2,8,128,128]{4,3,2,1,0:T(8,128)S(1)} %copy-done, f32[8,128,128]{2,1,0:T(8,128)S(1)} %copy-done.1), custom_call_target="tpu_custom_call" | custom-call | flops 13107200 | bytes 3145728 | tf_op jit(solution)/shard_map/inner/pallas_call | solution.py:132
  21.4 4.7 %collective-permute-done.refs_1_ = f32[2,6,128,128]{3,2,1,0:T(8,128)} collective-permute-done((f32[2,6,128,128]{3,2,1,0:T(8,128)}, f32[2,6,128,128]{3,2,1,0:T(8,128)}, u32[]{:S(2)}, u32[]{:S(2)}) %collective-permute-start) | collective-permute-done | bytes 786464 | tf_op jit(solution)/shard_map/ppermute | solution.py:347
  26.1 0.0 collective-permute-done.1.refs_2_
  26.1 1.9 %outer.2.refs_3_ = f32[2,8,128,128]{3,2,1,0:T(8,128)S(1)} custom-call(f32[2,8,128,128]{3,2,1,0:T(8,128)S(1)} %inner.2.refs_0_, f32[2,6,128,128]{3,2,1,0:T(8,128)} %collective-permute-done.refs_1_, f32[2,6,128,128]{3,2,1,0:T(8,128)} %collective-permute-done.1.refs_2_), custom_call_target="tpu_custom_call" | custom-call | flops 26214400000 | bytes 4194304 | tf_op jit(solution)/shard_map/outer/pallas_call | solution.py:159
  28.0 0.0 copy-start.2
  28.0 0.2 fusion
  28.2 0.2 collective-permute-start.3
  28.4 0.5 collective-permute-start.2
  28.9 0.1 copy-done.2
  29.1 4.1 %inner.3.refs_0_ = f32[2,8,128,128]{3,2,1,0:T(8,128)S(1)} custom-call(s32[1]{0:T(128)S(6)} %copy.5.refs_0_.index_ref, f32[3,2,8,128,128]{4,3,2,1,0:T(8,128)S(1)} %copy-done, f32[8,128,128]{2,1,0:T(8,128)S(1)} %copy-done.2, f32[2,8,128,128]{3,2,1,0:T(8,128)S(1)} %outer.2.refs_3_), custom_call_target="tpu_custom_call" | custom-call | flops 13107200 | bytes 3145728 | tf_op jit(solution)/shard_map/inner/pallas_call | solution.py:132
  33.1 10.1 %collective-permute-done.3.refs_2_ = f32[2,6,128,128]{3,2,1,0:T(8,128)S(1)} collective-permute-done((f32[2,6,128,128]{3,2,1,0:T(8,128)S(1)}, f32[2,6,128,128]{3,2,1,0:T(8,128)S(1)}, u32[]{:S(2)}, u32[]{:S(2)}) %collective-permute-start.3) | collective-permute-done | bytes 786464 | tf_op jit(solution)/shard_map/ppermute | solution.py:347
  43.3 5.9 %collective-permute-done.2.refs_1_ = f32[2,6,128,128]{3,2,1,0:T(8,128)S(1)} collective-permute-done((f32[2,6,128,128]{3,2,1,0:T(8,128)S(1)}, f32[2,6,128,128]{3,2,1,0:T(8,128)S(1)}, u32[]{:S(2)}, u32[]{:S(2)}) %collective-permute-start.2) | collective-permute-done | bytes 786464 | tf_op jit(solution)/shard_map/ppermute | solution.py:347
  49.2 2.7 %outer.3 = (f32[2,8,128,128]{3,2,1,0:T(8,128)}, f32[2,4,4,2,64,128]{5,4,3,2,1,0:T(8,128)S(1)}) custom-call(f32[2,8,128,128]{3,2,1,0:T(8,128)S(1)} %inner.3.refs_0_, f32[2,6,128,128]{3,2,1,0:T(8,128)S(1)} %collective-permute-done.2.refs_1_, f32[2,6,128,128]{3,2,1,0:T(8,128)S(1)} %collective-permute-done.3.refs_2_), custom_call_target="tpu_custom_call" | custom-call | flops 2621440 | bytes 4194304 | tf_op jit(solution)/shard_map/outer/pallas_call | solution.py:159
  51.9 0.0 copy-start.3
  51.9 1.4 copy-done.3
  53.2 2.1 %all-to-all-done = f32[16,6,64,128]{3,2,1,0:T(8,128)} async-done(((f32[16,6,64,128]{3,2,1,0:T(8,128)}), f32[16,6,64,128]{3,2,1,0:T(8,128)}, u32[]{:S(2)}, u32[]{:S(2)}) %all-to-all-start) | async-done | bytes 3145760 | tf_op jit(solution)/shard_map/all_to_all | solution.py:369
  55.3 35.9 %all_to_all.20 = f32[32,2,64,128]{3,2,1,0:T(8,128)S(1)} all-to-all(f32[32,2,64,128]{3,2,1,0:T(8,128)} %bitcast.10), channel_id=1, replica_groups=mesh['z'=4,'x'=4,'yl'=2,'yh'=2,'c'=2] {'yl','z','x'}, dimensions={0} | all-to-all | bytes 4194304 | tf_op jit(solution)/shard_map/all_to_all | solution.py:378
  91.3 4.3 %gram.1 = f32[48,128]{1,0:T(8,128)S(1)} custom-call(f32[96,64,128]{2,1,0:T(8,128)} %bitcast.1.panel_ref, f32[64,64,128]{2,1,0:T(8,128)S(1)} %bitcast.7), custom_call_target="tpu_custom_call" | custom-call | flops 301989888 | bytes 5242880 | tf_op jit(solution)/shard_map/gram/pallas_call | solution.py:286
  95.6 2.2 %collective-permute-start.6 = (f32[48,128]{1,0:T(8,128)S(1)}, f32[48,128]{1,0:T(8,128)S(1)}, u32[]{:S(2)}, u32[]{:S(2)}) collective-permute-start(f32[48,128]{1,0:T(8,128)S(1)} %gram.1), channel_id=1, source_target_pairs={{0,3},{1,2},{2,1},{3,0},{4,7},{5,6},{6,5},{7,4},{8,11},{9,10},{10,... | collective-permute-start | bytes 73736 | tf_op jit(solution)/shard_map/ppermute | solution.py:353
  97.7 3.3 %collective-permute-start.5 = (f32[48,128]{1,0:T(8,128)S(1)}, f32[48,128]{1,0:T(8,128)S(1)}, u32[]{:S(2)}, u32[]{:S(2)}) collective-permute-start(f32[48,128]{1,0:T(8,128)S(1)} %gram.1), channel_id=1, source_target_pairs={{0,2},{1,3},{2,0},{3,1},{4,6},{5,7},{6,4},{7,5},{8,10},{9,11},{10,... | collective-permute-start | bytes 73736 | tf_op jit(solution)/shard_map/ppermute | solution.py:353
  101.0 0.0 collective-permute-start.4
  101.0 0.0 collective-permute-done.6
  101.0 2.0 %collective-permute-done.5 = f32[48,128]{1,0:T(8,128)S(1)} collective-permute-done((f32[48,128]{1,0:T(8,128)S(1)}, f32[48,128]{1,0:T(8,128)S(1)}, u32[]{:S(2)}, u32[]{:S(2)}) %collective-permute-start.5) | collective-permute-done | bytes 24608 | tf_op jit(solution)/shard_map/ppermute | solution.py:353
  103.1 0.0 collective-permute-done.4
  103.1 15.9 %all_to_all.21.refs_0_ = f32[16,48,128]{2,1,0:T(8,128)S(1)} all-to-all(f32[16,48,128]{2,1,0:T(8,128)S(1)} %broadcast_in_dim.2), channel_id=1, replica_groups=mesh['z'=4,'x'=4,'yl'=2,'yh'=2,'c'=2] {'x','z'}, dimensions={0} | all-to-all | bytes 786432 | tf_op jit(solution)/shard_map/all_to_all | solution.py:356
  119.0 3.6 %project.1 = f32[96,64,128]{2,1,0:T(8,128)S(1)} custom-call(f32[16,48,128]{2,1,0:T(8,128)S(1)} %all_to_all.21.refs_0_, f32[64,64,128]{2,1,0:T(8,128)S(1)} %bitcast.8), custom_call_target="tpu_custom_call" | custom-call | flops 301989888 | bytes 5242880 | tf_op jit(solution)/shard_map/project/pallas_call | solution.py:330
  122.6 42.7 %all_to_all.22.change_ref = f32[16,6,64,128]{3,2,1,0:T(8,128)S(1)} all-to-all(f32[16,6,64,128]{3,2,1,0:T(8,128)S(1)} %bitcast.9), channel_id=1, replica_groups=mesh['z'=4,'x'=4,'yl'=2,'yh'=2,'c'=2] {'x','z'}, dimensions={0} | all-to-all | bytes 6291456 | tf_op jit(solution)/shard_map/all_to_all | solution.py:385
  165.4 1.8 %settle.1 = f32[6,16,64,128]{3,2,1,0:T(8,128)} custom-call(f32[6,16,64,128]{3,2,1,0:T(8,128)S(1)} %bitcast.6, f32[16,6,64,128]{3,2,1,0:T(8,128)S(1)} %all_to_all.22.change_ref), custom_call_target="tpu_custom_call" | custom-call | flops 786432 | bytes 9437184 | tf_op jit(solution)/shard_map/settle/pallas_call | solution.py:227
  (2 shorter events, 0.0 us)
Async XLA Ops:
  4.8 21.3 %collective-permute-start = (f32[2,6,128,128]{3,2,1,0:T(8,128)}, f32[2,6,128,128]{3,2,1,0:T(8,128)}, u32[]{:S(2)}, u32[]{:S(2)}) collective-permute-start(f32[2,6,128,128]{3,2,1,0:T(8,128)} %get-tuple-element.9), channel_id=1, source_target_pairs={{0,1},{1,2},{2,3},{3,0},{4,5},{5,6},{6,7},{7,4},{8,9},{9,10},{10,1... | collective-permute-start | bytes 2359304 | tf_op jit(solution)/shard_map/ppermute | solution.py:347
  4.9 21.2 %collective-permute-start.1 = (f32[2,6,128,128]{3,2,1,0:T(8,128)}, f32[2,6,128,128]{3,2,1,0:T(8,128)}, u32[]{:S(2)}, u32[]{:S(2)}) collective-permute-start(f32[2,6,128,128]{3,2,1,0:T(8,128)} %get-tuple-element.10), channel_id=1, source_target_pairs={{1,0},{2,1},{3,2},{0,3},{5,4},{6,5},{7,6},{4,7},{9,8},{10,9},{11,1... | collective-permute-start | bytes 2359304 | tf_op jit(solution)/shard_map/ppermute | solution.py:347
  8.1 8.2 %copy-start = (f32[3,2,8,128,128]{4,3,2,1,0:T(8,128)S(1)}, f32[3,2,8,128,128]{4,3,2,1,0:T(8,128)}, u32[]{:S(2)}) copy-start(f32[3,2,8,128,128]{4,3,2,1,0:T(8,128)} %refs_1_.3) | copy-start | bytes 9437188
  8.1 47.2 %all-to-all-start = ((f32[16,6,64,128]{3,2,1,0:T(8,128)}), f32[16,6,64,128]{3,2,1,0:T(8,128)}, u32[]{:S(2)}, u32[]{:S(2)}) async-start(f32[16,6,64,128]{3,2,1,0:T(8,128)} %get-tuple-element.13), calls=%async_computation | async-start | bytes 6291456 | tf_op jit(solution)/shard_map/all_to_all | solution.py:369
  16.3 1.0 copy-start.1
  28.0 1.0 copy-start.2
  28.2 15.1 %collective-permute-start.3 = (f32[2,6,128,128]{3,2,1,0:T(8,128)S(1)}, f32[2,6,128,128]{3,2,1,0:T(8,128)S(1)}, u32[]{:S(2)}, u32[]{:S(2)}) collective-permute-start(f32[2,6,128,128]{3,2,1,0:T(8,128)S(1)} %get-tuple-element.16), channel_id=1, source_target_pairs={{1,0},{2,1},{3,2},{0,3},{5,4},{6,5},{7,6},{4,7},{9,8},{10,9},{11,1... | collective-permute-start | bytes 2359304 | tf_op jit(solution)/shard_map/ppermute | solution.py:347
  28.4 20.8 %collective-permute-start.2 = (f32[2,6,128,128]{3,2,1,0:T(8,128)S(1)}, f32[2,6,128,128]{3,2,1,0:T(8,128)S(1)}, u32[]{:S(2)}, u32[]{:S(2)}) collective-permute-start(f32[2,6,128,128]{3,2,1,0:T(8,128)S(1)} %get-tuple-element.17), channel_id=1, source_target_pairs={{0,1},{1,2},{2,3},{3,0},{4,5},{5,6},{6,7},{7,4},{8,9},{9,10},{10,1... | collective-permute-start | bytes 2359304 | tf_op jit(solution)/shard_map/ppermute | solution.py:347
  51.9 1.4 copy-start.3
  95.6 5.5 %collective-permute-start.6 = (f32[48,128]{1,0:T(8,128)S(1)}, f32[48,128]{1,0:T(8,128)S(1)}, u32[]{:S(2)}, u32[]{:S(2)}) collective-permute-start(f32[48,128]{1,0:T(8,128)S(1)} %gram.1), channel_id=1, source_target_pairs={{0,3},{1,2},{2,1},{3,0},{4,7},{5,6},{6,5},{7,4},{8,11},{9,10},{10,... | collective-permute-start | bytes 73736 | tf_op jit(solution)/shard_map/ppermute | solution.py:353
  97.7 5.3 %collective-permute-start.5 = (f32[48,128]{1,0:T(8,128)S(1)}, f32[48,128]{1,0:T(8,128)S(1)}, u32[]{:S(2)}, u32[]{:S(2)}) collective-permute-start(f32[48,128]{1,0:T(8,128)S(1)} %gram.1), channel_id=1, source_target_pairs={{0,2},{1,3},{2,0},{3,1},{4,6},{5,7},{6,4},{7,5},{8,10},{9,11},{10,... | collective-permute-start | bytes 73736 | tf_op jit(solution)/shard_map/ppermute | solution.py:353
  101.0 2.0 %collective-permute-start.4 = (f32[48,128]{1,0:T(8,128)S(1)}, f32[48,128]{1,0:T(8,128)S(1)}, u32[]{:S(2)}, u32[]{:S(2)}) collective-permute-start(f32[48,128]{1,0:T(8,128)S(1)} %gram.1), channel_id=1, source_target_pairs={{0,1},{1,0},{2,3},{3,2},{4,5},{5,4},{6,7},{7,6},{8,9},{9,8},{10,11... | collective-permute-start | bytes 73736 | tf_op jit(solution)/shard_map/ppermute | solution.py:353
